TPU v7x, 32 devices: a whole 2x2x4 slice. The times are simulated.
32 devices in a mesh: dom: 32 (over z, y, x, core).
Axes of the slice: x: 2, y: 2, z: 4, core: 2. Of those that a mesh axis runs over, the one named last changes fastest.
Arguments:
- velocity: float32 [3, 3, 512, 512], P(None, None, 'dom'), may hold values from -6 to 6
- conv_past: float32 [2, 3, 512, 512], P(None, None, 'dom'), may hold values from -0.6 to 0.6
- metric: float32 [3, 512, 512], P(None, 'dom'), may hold values from 0.5 to 2
- jacobian: float32 [512, 512], P('dom'), may hold values from 0.5 to 2
- element_slot: int32 [512], P('dom'), may hold values from 0 to 15, as said below
Outputs:
- pressure: float32 [256, 896], P('dom')
- residual: float32 [256, 896], P('dom')
Inputs may be any that keep to these rules, and one draw needn't show every extreme that they name: `element_slot`: within each aligned block of 16 entries (one slab's elements) the entries are a permutation of 0 to 15.
All inputs are finite; a program needn't handle non-finite values.
Results may differ from a plain program's by a relative error of at most 0.0003.
Values sent between devices are 32-bit elements; how exact they have to be, the bound alone decides.
A program may use at most 64 MiB of HBM per device.

v0:
```python
import functools

import jax
import jax.numpy as jnp
import numpy as np
from jax import lax
from jax.experimental import pallas as pl
from jax.experimental.pallas import tpu as pltpu
from jax.sharding import PartitionSpec as P

NP = 8
NF = 12
ES = 16
ITERS = 3
A0 = 8
A1 = 112
A2 = 8
ROUNDS = 8
LANES = 128
MESH = pl.DeviceIdType.MESH

time_step = 0.25
viscosity = 0.05
mass_shift = 0.001


def legendre_pair(points, order):
    before = np.ones(points.shape)
    current = points * 1.0
    for level in range(2, order + 1):
        nextone = ((2 * level - 1) * points * current - (level - 1) * before) / level
        before = current
        current = nextone
    return (current, before)


def jacobi_eigen(matrix):
    size = matrix.shape[0]
    work = matrix * 1.0
    vectors = np.eye(size)
    for sweep in range(30):
        for first in range(size - 1):
            for second in range(first + 1, size):
                off = float(work[first, second])
                if abs(off) > 1e-300:
                    tau = (float(work[second, second]) - float(work[first, first])) / (2.0 * off)
                    if tau >= 0.0:
                        tangent = 1.0 / (tau + (1.0 + tau * tau) ** 0.5)
                    else:
                        tangent = -1.0 / (-tau + (1.0 + tau * tau) ** 0.5)
                    cosine = 1.0 / (1.0 + tangent * tangent) ** 0.5
                    sine = tangent * cosine
                    rotation = np.eye(size)
                    rotation[first, first] = cosine
                    rotation[second, second] = cosine
                    rotation[first, second] = sine
                    rotation[second, first] = -sine
                    work = rotation.T @ work @ rotation
                    vectors = vectors @ rotation
    diagonal_index = np.arange(size)
    return (work[diagonal_index, diagonal_index], vectors)


def build_tables(points_edge, points_fine):
    degree = points_edge - 1
    points = -np.cos(np.pi * np.arange(points_edge) / degree)
    for sweep in range(100):
        top, below = legendre_pair(points, degree)
        points = points - (points * top - below) / (points_edge * top)
    top, below = legendre_pair(points, degree)
    weight_gll = 2.0 / (degree * points_edge * top**2)
    spacing = points[:, None] - points[None, :] + np.eye(points_edge)
    barycentric = 1.0 / np.prod(spacing, axis=1)
    derivative = barycentric[None, :] / barycentric[:, None] / spacing
    derivative = derivative * (1.0 - np.eye(points_edge))
    derivative = derivative - np.eye(points_edge) * derivative.sum(axis=1)[:, None]
    fine_points = np.cos(np.pi * (np.arange(points_fine) + 0.75) / (points_fine + 0.5))
    for sweep in range(100):
        top, below = legendre_pair(fine_points, points_fine)
        slope = points_fine * (fine_points * top - below) / (fine_points * fine_points - 1.0)
        fine_points = fine_points - top / slope
    top, below = legendre_pair(fine_points, points_fine)
    slope = points_fine * (fine_points * top - below) / (fine_points * fine_points - 1.0)
    fine_weight = 2.0 / ((1.0 - fine_points * fine_points) * slope * slope)
    fine_points = fine_points[::-1]
    fine_weight = fine_weight[::-1]
    interpolate = np.ones((points_fine, points_edge))
    for column in range(points_edge):
        for other in range(points_edge):
            if other != column:
                interpolate[:, column] = (
                    interpolate[:, column]
                    * (fine_points - points[other])
                    / (points[column] - points[other])
                )
    stiffness = derivative.T @ (weight_gll[:, None] * derivative)
    extent = 3 * degree + 1
    joined_stiff = np.zeros((extent, extent))
    joined_mass = np.zeros(extent)
    for segment in range(3):
        offset = segment * degree
        joined_stiff[offset : offset + points_edge, offset : offset + points_edge] += stiffness
        joined_mass[offset : offset + points_edge] += weight_gll
    low = degree - 1
    high = 2 * degree + 2
    root_mass = np.sqrt(joined_mass[low:high])
    scaled = joined_stiff[low:high, low:high] / root_mass[:, None] / root_mass[None, :]
    scaled = 0.5 * (scaled + scaled.T)
    eigen_values, eigen_vectors = jacobi_eigen(scaled)
    solve_mat = eigen_vectors / root_mass[:, None]
    breadth = high - low
    identity = np.eye(points_edge)
    operator_tables = {
        "derivative": derivative,
        "dpair": np.concatenate(
            [np.kron(derivative, identity).T, np.kron(identity, derivative).T], axis=1
        ),
        "interpolate": interpolate,
        "ipair": np.kron(interpolate, interpolate).T,
        "mass_three": (
            weight_gll[:, None, None] * weight_gll[None, :, None] * weight_gll[None, None, :]
        ).reshape(points_edge, points_edge * points_edge),
        "fine_three": (
            fine_weight[:, None, None] * fine_weight[None, :, None] * fine_weight[None, None, :]
        ).reshape(points_fine, points_fine * points_fine),
        "solve_mat": solve_mat,
        "solve_pair": np.kron(solve_mat, solve_mat),
        "eigen_axial": eigen_values,
        "eigen_around": np.repeat(eigen_values, breadth),
        "eigen_radial": np.tile(eigen_values, breadth),
    }
    operator_tables["weight"] = weight_gll
    operator_tables["fine_weight"] = fine_weight
    return operator_tables


def split_rows(matrix):
    exact = np.asarray(matrix, np.float32)
    high = exact.astype(jnp.bfloat16)
    low = (exact - high.astype(np.float32)).astype(jnp.bfloat16)
    return np.concatenate([high, high, low], axis=0)


def halves(matrix):
    rows, columns = matrix.shape
    table = np.zeros((rows // 2, columns // 2, 2, LANES))
    for out in range(rows // 2):
        for into in range(columns // 2):
            table[out, into, 0, :64] = matrix[2 * out, 2 * into]
            table[out, into, 0, 64:] = matrix[2 * out + 1, 2 * into + 1]
            table[out, into, 1, :64] = matrix[2 * out, 2 * into + 1]
            table[out, into, 1, 64:] = matrix[2 * out + 1, 2 * into]
    return np.asarray(table.reshape(-1, LANES), np.float32)


def twice(block, stride):
    rows, columns = block.shape
    result = np.zeros((2 * rows, 2 * stride))
    result[:rows, :columns] = block
    result[rows:, stride : stride + columns] = block
    return result


def pad_columns(matrix, total):
    return np.pad(matrix, ((0, 0), (0, total - matrix.shape[1])))


def by_tile(table):
    return np.asarray(np.repeat(table.reshape(-1, LANES), ES, axis=0), np.float32)


@functools.cache
def constants():
    t = build_tables(NP, NF)
    d, itp, s = t["derivative"], t["interpolate"], t["solve_mat"]
    eye = np.eye(NP)
    pair = np.concatenate(
        [twice(np.kron(d, eye).T, 64), twice(np.kron(eye, d).T, 64)], axis=1
    )
    fine = pad_columns(twice(np.kron(itp, itp).T, 144), 384)
    slope = itp @ d
    fine_slope = np.concatenate(
        [
            pad_columns(twice(np.kron(slope, itp).T, 144), 384),
            pad_columns(twice(np.kron(itp, slope).T, 144), 384),
        ],
        axis=1,
    )
    inner = s[1:9]
    ahead = np.zeros((2 * LANES, 2 * LANES))
    back = np.zeros((2 * LANES, 2 * LANES))
    for h in range(2):
        out = slice(h * LANES, h * LANES + 100)

        def lanes(row):
            return slice(h * 64 + row * 8, h * 64 + row * 8 + 8)

        def beside(row):
            return slice(LANES + h * 64 + row * 8, LANES + h * 64 + row * 8 + 8)

        for row in range(NP):
            ahead[lanes(row), out] = np.kron(s[row + 1 : row + 2], inner)
            back[lanes(row), out] = np.kron(s[row + 1 : row + 2], inner)
        ahead[beside(6), out] = np.kron(s[0:1], inner)
        ahead[beside(1), out] = np.kron(s[9:10], inner)
        back[beside(0), out] = np.kron(s[8:9], inner)
        back[beside(1), out] = np.kron(s[9:10], inner)
        back[beside(7), out] = np.kron(s[1:2], inner)
        back[beside(6), out] = np.kron(s[0:1], inner)
    wf = t["fine_weight"]
    wf2 = (wf[:, None] * wf[None, :]).reshape(-1)
    fine_mass = np.zeros((6, 384))
    for j in range(6):
        fine_mass[j, :144] = wf[2 * j] * wf2
        fine_mass[j, 144:288] = wf[2 * j + 1] * wf2
    eigen = np.zeros((2, LANES))
    eigen[0, :100] = t["eigen_around"]
    eigen[1, :100] = t["eigen_radial"]
    share = np.ones((NP, NP, NP))
    share[0] *= 0.5
    share[-1] *= 0.5
    share[:, 0] *= 0.5
    share[:, -1] *= 0.5
    nodes = np.stack([by_tile(t["mass_three"]), by_tile(share)])
    arrays = [
        split_rows(pair),
        split_rows(pair.T),
        split_rows(fine),
        split_rows(fine_slope),
        split_rows(fine.T),
        split_rows(ahead),
        split_rows(back.T),
        np.concatenate([halves(d), halves(d.T), halves(itp), halves(slope), halves(itp.T)]),
        nodes,
        np.asarray(np.repeat(fine_mass, ES, axis=0), np.float32),
        np.asarray(eigen, np.float32),
    ]
    return arrays, np.asarray(s, np.float32), np.asarray(t["eigen_axial"], np.float32)


COEF_D, COEF_DT, COEF_I, COEF_S, COEF_IT = 0, 32, 64, 112, 160


def stages_of(count):
    stages = []
    stride = 1
    while stride < count:
        size = min(8, count // stride)
        while (count // stride) % size:
            size -= 1
        stages.append((stride, size))
        stride *= size
    return stages


def kernel(
    count,
    velocity,
    past,
    metric,
    jacobian,
    slots,
    w_pair,
    w_pair_t,
    w_fine,
    w_slope,
    w_fine_t,
    w_ahead,
    w_back,
    coef,
    nodes,
    fine_mass,
    eigen,
    pressure_ref,
    residual_ref,
    send_left,
    send_right,
    from_left,
    from_right,
    gathered,
    turned,
    send_left_sem,
    send_right_sem,
    from_left_sem,
    from_right_sem,
    gather_send_sem,
    gather_recv_sem,
):
    _, solve, eigen_axial = constants()
    me = lax.axis_index("dom")
    left = lax.rem(me + count - 1, count)
    right = lax.rem(me + 1, count)
    stages = stages_of(count)

    def peer(stage, offset):
        stride, size = stages[stage]
        digit = lax.rem(me // stride, size)
        other = lax.rem(digit + offset, size)
        return me + (other - digit) * stride

    barrier = pltpu.get_barrier_semaphore()
    greeted = [left, right] + [
        peer(stage, offset)
        for stage in range(len(stages))
        for offset in range(1, stages[stage][1])
    ]
    for other in greeted:
        pl.semaphore_signal(barrier, inc=1, device_id=(other,), device_id_type=MESH)

    lane = lax.broadcasted_iota(jnp.int32, (ES, LANES), 1)
    low = lane < 64
    node_s = lax.rem(lane, 64) // 8

    def tiles(field):
        return [field[i * ES : (i + 1) * ES] for i in range(field.shape[0] // ES)]

    def stack(parts):
        return jnp.concatenate(parts, axis=0)

    def mm(x, w):
        high = x.astype(jnp.bfloat16)
        rest = (x - high.astype(jnp.float32)).astype(jnp.bfloat16)
        return jnp.dot(
            jnp.concatenate([high, rest, high], axis=1), w[...], preferred_element_type=jnp.float32
        )

    def swap(tile):
        return pltpu.roll(tile, 64, 1)

    def along(field, base, total):
        parts = tiles(field)
        swapped = [swap(part) for part in parts]
        results = []
        for out in range(total):
            acc = None
            for into in range(len(parts)):
                at = base + 2 * (out * len(parts) + into)
                term = coef[at : at + 1] * parts[into] + coef[at + 1 : at + 2] * swapped[into]
                acc = term if acc is None else acc + term
            results.append(acc)
        return stack(results)

    def gradient(field):
        paired = mm(field, w_pair)
        return along(field, COEF_D, 4), paired[:, :LANES], paired[:, LANES:]

    def gradient_t(axial, around, radial):
        paired = mm(jnp.concatenate([around, radial], axis=1), w_pair_t)
        return paired + along(axial, COEF_DT, 4)

    def before(tile):
        return pltpu.roll(tile, 1, 0)

    def after(tile):
        return pltpu.roll(tile, ES - 1, 0)

    def around_sum(field):
        results = []
        for tile in tiles(field):
            first = before(pltpu.roll(tile, 72, 1))
            last = after(pltpu.roll(tile, 56, 1))
            results.append(
                tile + jnp.where(node_s == 0, first, jnp.where(node_s == 7, last, 0.0))
            )
        return stack(results)

    def copies(step):
        at, size = (0, 4 * ES) if step == 0 else ((3 + step) * ES, ES)
        rows = pl.ds(at, size)
        to_left = pltpu.make_async_remote_copy(
            src_ref=send_left.at[rows],
            dst_ref=from_right.at[rows],
            send_sem=send_left_sem.at[step],
            recv_sem=from_right_sem.at[step],
            device_id=(left,),
            device_id_type=MESH,
        )
        to_right = pltpu.make_async_remote_copy(
            src_ref=send_right.at[rows],
            dst_ref=from_left.at[rows],
            send_sem=send_right_sem.at[step],
            recv_sem=from_left_sem.at[step],
            device_id=(right,),
            device_id_type=MESH,
        )
        return rows, to_left, to_right

    def exchange(step, for_left, for_right):
        rows, to_left, to_right = copies(step)
        send_left[rows] = for_left
        to_left.start()
        send_right[rows] = for_right
        to_right.start()
        to_right.wait_recv()
        to_left.wait_recv()
        return from_left[rows], from_right[rows]

    def axial_sum(step, fields):
        parts = [tiles(field) for field in fields]
        lefts, rights = exchange(
            step, stack([p[0] for p in parts]), stack([p[3] for p in parts])
        )
        lefts, rights = tiles(lefts), tiles(rights)
        results = []
        for p, far_left, far_right in zip(parts, lefts, rights):
            results.append(
                stack(
                    [
                        p[0] + jnp.where(low, swap(far_left), 0.0),
                        p[1],
                        p[2],
                        p[3] + jnp.where(low, 0.0, swap(far_right)),
                    ]
                )
            )
        return results, jnp.where(low, lefts[0], rights[0])

    def element_field(ref, *index):
        return stack([ref[index + (slice(None), pl.ds(j * LANES, LANES))] for j in range(4)])

    weight3, share = nodes[0], nodes[1]
    jac = element_field(jacobian)
    mass = jac * weight3
    metrics = [element_field(metric, d) for d in range(3)]
    squares = [mass * m * m for m in metrics]
    newest = [element_field(velocity, 0, i) for i in range(3)]
    coarse = [along(jac, COEF_I, 6)]
    coarse += [along(newest[d] * metrics[d], COEF_I, 6) for d in range(3)]
    coarse += [along(newest[i], COEF_S, 6) for i in range(3)]
    fine = mm(stack(coarse), w_fine)
    fine = [fine[i * 96 : (i + 1) * 96] for i in range(7)]
    crossed = mm(stack([along(newest[i], COEF_I, 6) for i in range(3)]), w_slope)
    fine_jac = fine[0] * fine_mass[...]
    products = []
    for i in range(3):
        rows = slice(i * 96, (i + 1) * 96)
        products.append(
            fine_jac
            * (
                fine[1] * fine[4 + i]
                + fine[2] * crossed[rows, :384]
                + fine[3] * crossed[rows, 384:]
            )
        )
    advected = mm(stack(products), w_fine_t)
    guessed = [
        3.0 * newest[i] - 3.0 * element_field(velocity, 1, i) + element_field(velocity, 2, i)
        for i in range(3)
    ]
    paired = mm(stack(guessed), w_pair)
    slopes = jnp.concatenate(
        [
            stack([squares[1] * paired[i * 64 : (i + 1) * 64, :LANES] for i in range(3)]),
            stack([squares[2] * paired[i * 64 : (i + 1) * 64, LANES:] for i in range(3)]),
        ],
        axis=1,
    )
    paired_t = mm(slopes, w_pair_t)
    forcing = []
    for i in range(3):
        convect = along(advected[i * 96 : (i + 1) * 96], COEF_IT, 4)
        stiff = paired_t[i * 64 : (i + 1) * 64] + along(
            squares[0] * along(guessed[i], COEF_D, 4), COEF_DT, 4
        )
        history = (
            3.0 * newest[i]
            - 1.5 * element_field(velocity, 1, i)
            + element_field(velocity, 2, i) / 3.0
        )
        extrap = (
            3.0 * convect - 3.0 * element_field(past, 0, i) + element_field(past, 1, i)
        )
        helmholtz = viscosity * stiff + 11.0 / (6.0 * time_step) * mass * guessed[i]
        forcing.append(mass * history / time_step - extrap - helmholtz)

    fields = forcing + [mass] + metrics
    wide = jnp.concatenate([tile for field in fields for tile in tiles(field)], axis=1)
    first = wide.astype(jnp.bfloat16)
    rest = wide - first.astype(jnp.float32)
    second = rest.astype(jnp.bfloat16)
    third = (rest - second.astype(jnp.float32)).astype(jnp.bfloat16)
    position = lax.broadcasted_iota(jnp.int32, (ES, 3 * ES), 0)
    chosen = jnp.where(slots[...] == position, 1.0, 0.0).astype(jnp.bfloat16)
    placed = jnp.dot(chosen, stack([first, second, third]), preferred_element_type=jnp.float32)
    fields = [
        stack([placed[:, (4 * f + j) * LANES : (4 * f + j + 1) * LANES] for j in range(4)])
        for f in range(7)
    ]
    forcing, mass, metrics = fields[:3], fields[3], fields[4:]
    lumps = [mass * m for m in metrics]
    squares = [lumps[d] * metrics[d] for d in range(3)]

    def total(field):
        parts = tiles(field)
        return jnp.sum(parts[0] + parts[1] + parts[2] + parts[3], axis=1, keepdims=True) / 8.0

    scales = [total(square) for square in squares]
    flat = (
        scales[1] * eigen[0:1] + scales[2] * eigen[1:2] + mass_shift * total(mass)
    )
    inverse = [1.0 / (scales[0] * float(eigen_axial[k]) + flat) for k in range(10)]

    pl.semaphore_wait(barrier, len(greeted))
    summed, _ = axial_sum(0, [around_sum(f) for f in forcing + [mass]])
    accel = [lumps[d] * (summed[d] / summed[3]) for d in range(3)]
    divergence = around_sum(gradient_t(accel[0], accel[1], accel[2]))
    (source,), source_halo = axial_sum(1, [divergence])

    def smooth(step, field, halo):
        parts = tiles(field) + [halo]
        sides = [
            jnp.where(node_s == 6, before(p), jnp.where(node_s == 1, after(p), 0.0))
            for p in parts
        ]
        modes = mm(jnp.concatenate([stack(parts), stack(sides)], axis=1), w_ahead)
        rows = tiles(modes)
        order = [rows[4][:, :LANES]]
        for j in range(4):
            order += [rows[j][:, :LANES], rows[j][:, LANES:]]
        order.append(rows[4][:, LANES:])
        spectra = []
        for k in range(10):
            acc = order[0] * float(solve[0, k])
            for a in range(1, 10):
                acc = acc + order[a] * float(solve[a, k])
            spectra.append(acc * inverse[k])
        restored = []
        for a in range(10):
            acc = spectra[0] * float(solve[a, 0])
            for k in range(1, 10):
                acc = acc + spectra[k] * float(solve[a, k])
            restored.append(acc)
        lows = [restored[1], restored[3], restored[5], restored[7], restored[0]]
        highs = [restored[2], restored[4], restored[6], restored[8], restored[9]]
        given = mm(jnp.concatenate([stack(lows), stack(highs)], axis=1), w_back)
        own, other = tiles(given[:, :LANES]), tiles(given[:, LANES:])
        own = [
            o + jnp.where(node_s <= 1, before(n), jnp.where(node_s >= 6, after(n), 0.0))
            for o, n in zip(own, other)
        ]
        far_left, far_right = exchange(
            step,
            jnp.where(low, own[4], swap(own[0])),
            jnp.where(low, swap(own[3]), own[4]),
        )
        return stack([own[0] + far_left, own[1], own[2], own[3] + far_right])

    def apply(step, field):
        axial, around, radial = gradient(field)
        local = gradient_t(squares[0] * axial, squares[1] * around, squares[2] * radial)
        local = around_sum(local + mass_shift * mass * field)
        (image,), halo = axial_sum(step, [local])
        return image, halo

    def inner(one, two):
        return jnp.sum(one * two * share, axis=0, keepdims=True)

    spaces, images = [], []
    current, halo = source, source_halo
    for it in range(ITERS):
        spaces.append(smooth(2 + 2 * it, current, halo))
        current, halo = apply(3 + 2 * it, spaces[-1])
        images.append(current)

    pairs = [(source, spaces[0])] + [
        (images[i], spaces[j]) for i in range(3) for j in range(i, 3)
    ]
    value = jnp.concatenate([inner(x, y) for x, y in pairs] + [jnp.zeros((1, LANES))], axis=0)
    started = []
    for stage, (stride, size) in enumerate(stages):
        digit = lax.rem(me // stride, size)
        gathered[stage, digit] = value
        for offset in range(1, size):
            copy = pltpu.make_async_remote_copy(
                src_ref=gathered.at[stage, digit],
                dst_ref=gathered.at[stage, digit],
                send_sem=gather_send_sem.at[stage, offset],
                recv_sem=gather_recv_sem.at[stage, offset],
                device_id=(peer(stage, offset),),
                device_id_type=MESH,
            )
            copy.start()
            started.append(copy)
        for copy in started[1 - size :]:
            copy.wait_recv()
        value = gathered[stage, 0]
        for slot in range(1, size):
            value = value + gathered[stage, slot]
    sums = jnp.sum(value, axis=1, keepdims=True)
    sums = [sums[i : i + 1] for i in range(7)]
    gram = {}
    for at, (i, j) in enumerate([(i, j) for i in range(3) for j in range(i, 3)]):
        gram[i, j] = gram[j, i] = sums[1 + at]
    heads = [sums[0], gram[0, 0], gram[0, 1]]
    taken = [None] * 3
    direction = [None] * 3
    result = [None] * 3
    previous = None
    for it in range(ITERS):
        z = [None] * 3
        z[0] = jnp.ones((1, 1), jnp.float32)
        for k in range(1, it + 1):
            z[k] = taken[k - 1]
        rho = heads[0]
        for k in range(1, it + 1):
            rho = rho + z[k] * heads[k]
        for i in range(it):
            row = gram[i, 0]
            for k in range(1, it + 1):
                row = row + z[k] * gram[i, k]
            rho = rho + taken[i] * row
        if it == 0:
            direction = [z[0], None, None]
        else:
            beta = rho / previous
            direction = [
                None if k > it else z[k] if direction[k] is None else z[k] + beta * direction[k]
                for k in range(3)
            ]
        bottom = None
        for i in range(it + 1):
            row = None
            for k in range(it + 1):
                term = direction[k] * gram[i, k]
                row = term if row is None else row + term
            bottom = direction[i] * row if bottom is None else bottom + direction[i] * row
        alpha = rho / bottom
        for k in range(it + 1):
            step = alpha * direction[k]
            result[k] = step if result[k] is None else result[k] + step
            taken[k] = -step if taken[k] is None else taken[k] - step
        previous = rho
    final = [spaces[0] * result[0], source]
    for k in range(3):
        final[1] = final[1] + images[k] * taken[k]
        if k:
            final[0] = final[0] + spaces[k] * result[k]

    for which, ref in enumerate((pressure_ref, residual_ref)):
        for j, tile in enumerate(tiles(final[which])):
            turned[which, pl.ds(2 * j * ES, ES)] = tile
            turned[which, pl.ds((2 * j + 1) * ES, ES)] = swap(tile)
        for p in range(ES):
            block = turned[which, pl.ds(p, NP, stride=ES), :]
            ref[:, p * 56 : (p + 1) * 56] = block[:, :56]

    for step in range(ROUNDS):
        _, to_left, to_right = copies(step)
        to_left.wait_send()
        to_right.wait_send()
    for copy in started:
        copy.wait_send()


def shards(count, velocity, conv_past, metric, jacobian, element_slot):
    arrays, _, _ = constants()
    stages = stages_of(count)
    block = jax.ShapeDtypeStruct((A0, A1 * A2), jnp.float32)
    whole = pl.BlockSpec(memory_space=pltpu.VMEM)
    rows = (3 + ROUNDS) * ES
    slots = jnp.tile(element_slot, 3).reshape(1, 3 * ES)
    return pl.pallas_call(
        functools.partial(kernel, count),
        out_shape=(block, block),
        in_specs=[whole] * (5 + len(arrays)),
        out_specs=(whole, whole),
        scratch_shapes=[
            pltpu.VMEM((rows, LANES), jnp.float32),
            pltpu.VMEM((rows, LANES), jnp.float32),
            pltpu.VMEM((rows, LANES), jnp.float32),
            pltpu.VMEM((rows, LANES), jnp.float32),
            pltpu.VMEM((len(stages), 8, 8, LANES), jnp.float32),
            pltpu.VMEM((2, NP * ES, LANES), jnp.float32),
            pltpu.SemaphoreType.DMA((ROUNDS,)),
            pltpu.SemaphoreType.DMA((ROUNDS,)),
            pltpu.SemaphoreType.DMA((ROUNDS,)),
            pltpu.SemaphoreType.DMA((ROUNDS,)),
            pltpu.SemaphoreType.DMA((len(stages), 8)),
            pltpu.SemaphoreType.DMA((len(stages), 8)),
        ],
        compiler_params=pltpu.CompilerParams(
            collective_id=0, has_side_effects=True, vmem_limit_bytes=40 * 1024 * 1024
        ),
    )(velocity, conv_past, metric, jacobian, slots, *[jnp.asarray(a) for a in arrays])


def solution(mesh):
    return jax.shard_map(
        functools.partial(shards, mesh.shape["dom"]),
        mesh=mesh,
        in_specs=(
            P(None, None, "dom", None),
            P(None, None, "dom", None),
            P(None, "dom", None),
            P("dom", None),
            P("dom"),
        ),
        out_specs=(P("dom", None), P("dom", None)),
        check_vma=False,
    )
```

profile of v0, /device:TPU:0, one launch (start us, length us, event | category | flops | bytes accessed | tf_op | source)
XLA Modules:
  0.0 64.6 jit_solution(16752839679454567656)
XLA Ops:
  0.6 0.7 %tile.2 = s32[3,16]{1,0:T(4,128)S(1)} broadcast(s32[16]{0:T(128)} %param.20), dimensions={1} | broadcast | bytes 256 | tf_op jit(solution)/shard_map/tile | solution.py:661
  1.3 0.0 copy-start.14
  1.3 0.1 reshape_tile.3.slots
  1.4 0.6 copy-done.14
  2.0 0.0 copy-start
  2.0 1.1 %copy-done = bf16[384,768]{1,0:T(8,128)(2,1)S(1)} copy-done((bf16[384,768]{1,0:T(8,128)(2,1)S(1)}, bf16[384,768]{1,0:T(8,128)(2,1)}, u32[]{:S(2)}) %copy-start) | copy-done | bytes 589848
  3.0 0.0 copy-start.1
  3.0 1.0 %copy-done.1 = bf16[768,256]{1,0:T(8,128)(2,1)S(1)} copy-done((bf16[768,256]{1,0:T(8,128)(2,1)S(1)}, bf16[768,256]{1,0:T(8,128)(2,1)}, u32[]{:S(2)}) %copy-start.1) | copy-done | bytes 393240
  4.0 0.0 copy-start.2
  4.0 1.0 %copy-done.2 = bf16[768,256]{1,0:T(8,128)(2,1)S(1)} copy-done((bf16[768,256]{1,0:T(8,128)(2,1)S(1)}, bf16[768,256]{1,0:T(8,128)(2,1)}, u32[]{:S(2)}) %copy-start.2) | copy-done | bytes 393240
  5.0 0.0 copy-start.3
  5.0 1.0 %copy-done.3 = f32[3,3,16,512]{3,2,1,0:T(8,128)S(1)} copy-done((f32[3,3,16,512]{3,2,1,0:T(8,128)S(1)}, f32[3,3,16,512]{3,2,1,0:T(8,128)}, u32[]{:S(2)}) %copy-start.3) | copy-done | bytes 294936
  6.0 0.0 copy-start.4
  6.0 1.0 %copy-done.4 = bf16[1152,128]{1,0:T(8,128)(2,1)S(1)} copy-done((bf16[1152,128]{1,0:T(8,128)(2,1)S(1)}, bf16[1152,128]{1,0:T(8,128)(2,1)}, u32[]{:S(2)}) %copy-start.4) | copy-done | bytes 294936
  6.9 0.0 copy-start.5
  7.0 1.0 %copy-done.5 = bf16[384,384]{1,0:T(8,128)(2,1)S(1)} copy-done((bf16[384,384]{1,0:T(8,128)(2,1)S(1)}, bf16[384,384]{1,0:T(8,128)(2,1)}, u32[]{:S(2)}) %copy-start.5) | copy-done | bytes 294936
  7.9 0.9 %copy-done.6 = f32[2,3,16,512]{3,2,1,0:T(8,128)S(1)} copy-done((f32[2,3,16,512]{3,2,1,0:T(8,128)S(1)}, f32[2,3,16,512]{3,2,1,0:T(8,128)}, u32[]{:S(2)}) %copy-start.6) | copy-done | bytes 196632
  8.8 0.0 copy-start.7
  8.8 0.9 %copy-done.7 = bf16[768,128]{1,0:T(8,128)(2,1)S(1)} copy-done((bf16[768,128]{1,0:T(8,128)(2,1)S(1)}, bf16[768,128]{1,0:T(8,128)(2,1)}, u32[]{:S(2)}) %copy-start.7) | copy-done | bytes 196632
  9.8 0.0 copy-start.8
  9.8 0.9 %copy-done.8 = bf16[384,256]{1,0:T(8,128)(2,1)S(1)} copy-done((bf16[384,256]{1,0:T(8,128)(2,1)S(1)}, bf16[384,256]{1,0:T(8,128)(2,1)}, u32[]{:S(2)}) %copy-start.8) | copy-done | bytes 196632
  10.7 0.0 copy-start.9
  10.7 0.9 %copy-done.9 = f32[96,384]{1,0:T(8,128)S(1)} copy-done((f32[96,384]{1,0:T(8,128)S(1)}, f32[96,384]{1,0:T(8,128)}, u32[]{:S(2)}) %copy-start.9) | copy-done | bytes 147480
  11.6 0.0 copy-start.10
  11.6 0.9 %copy-done.10 = f32[208,128]{1,0:T(8,128)S(1)} copy-done((f32[208,128]{1,0:T(8,128)S(1)}, f32[208,128]{1,0:T(8,128)}, u32[]{:S(2)}) %copy-start.10) | copy-done | bytes 106520
  12.5 0.0 copy-start.11
  12.5 0.9 %copy-done.11 = f32[3,16,512]{2,1,0:T(8,128)S(1)} copy-done((f32[3,16,512]{2,1,0:T(8,128)S(1)}, f32[3,16,512]{2,1,0:T(8,128)}, u32[]{:S(2)}) %copy-start.11) | copy-done | bytes 98328
  13.4 0.8 %copy-done.12 = f32[2,64,128]{2,1,0:T(8,128)S(1)} copy-done((f32[2,64,128]{2,1,0:T(8,128)S(1)}, f32[2,64,128]{2,1,0:T(8,128)}, u32[]{:S(2)}) %copy-start.12) | copy-done | bytes 65560
  14.2 0.8 %copy-done.13 = f32[16,512]{1,0:T(8,128)S(1)} copy-done((f32[16,512]{1,0:T(8,128)S(1)}, f32[16,512]{1,0:T(8,128)}, u32[]{:S(2)}) %copy-start.13) | copy-done | bytes 32792
  15.0 48.4 %shard_map.167 = (f32[8,896]{1,0:T(8,128)S(1)}, f32[8,896]{1,0:T(8,128)S(1)}) custom-call(f32[3,3,16,512]{3,2,1,0:T(8,128)S(1)} %copy-done.3, f32[2,3,16,512]{3,2,1,0:T(8,128)S(1)} %copy-done.6, f32[3,16,512]{2,1,0:T(8,128)S(1)} %copy-done.11, f32[16,512]{1,0:T(8,128)S(1)} %copy-done.13, s32[1,48]{1,0:T(1,128)S(1)} %reshape_tile.3.slots, ...), custom_call_target="tpu_custom_call" | custom-call | tf_op jit(solution)/shard_map/pallas_call | solution.py:662
  63.4 0.6 copy.20
  64.0 0.6 copy.21
  (3 shorter events, 0.0 us)
Async XLA Ops:
  1.3 0.7 %copy-start.14 = (f32[2,128]{1,0:T(2,128)S(1)}, f32[2,128]{1,0:T(2,128)}, u32[]{:S(2)}) copy-start(f32[2,128]{1,0:T(2,128)} %constant.32.clone.eigen) | copy-start | bytes 3076
  2.0 1.1 %copy-start = (bf16[384,768]{1,0:T(8,128)(2,1)S(1)}, bf16[384,768]{1,0:T(8,128)(2,1)}, u32[]{:S(2)}) copy-start(bf16[384,768]{1,0:T(8,128)(2,1)} %constant.25.clone.w_slope) | copy-start | bytes 1769476
  3.0 1.0 %copy-start.1 = (bf16[768,256]{1,0:T(8,128)(2,1)S(1)}, bf16[768,256]{1,0:T(8,128)(2,1)}, u32[]{:S(2)}) copy-start(bf16[768,256]{1,0:T(8,128)(2,1)} %constant.28.clone.w_back) | copy-start | bytes 1179652
  4.0 1.0 %copy-start.2 = (bf16[768,256]{1,0:T(8,128)(2,1)S(1)}, bf16[768,256]{1,0:T(8,128)(2,1)}, u32[]{:S(2)}) copy-start(bf16[768,256]{1,0:T(8,128)(2,1)} %constant.27.clone.w_ahead) | copy-start | bytes 1179652
  5.0 1.0 %copy-start.3 = (f32[3,3,16,512]{3,2,1,0:T(8,128)S(1)}, f32[3,3,16,512]{3,2,1,0:T(8,128)}, u32[]{:S(2)}) copy-start(f32[3,3,16,512]{3,2,1,0:T(8,128)} %velocity.1) | copy-start | bytes 884740
  6.0 1.0 %copy-start.4 = (bf16[1152,128]{1,0:T(8,128)(2,1)S(1)}, bf16[1152,128]{1,0:T(8,128)(2,1)}, u32[]{:S(2)}) copy-start(bf16[1152,128]{1,0:T(8,128)(2,1)} %constant.26.clone.w_fine_t) | copy-start | bytes 884740
  6.9 1.0 %copy-start.5 = (bf16[384,384]{1,0:T(8,128)(2,1)S(1)}, bf16[384,384]{1,0:T(8,128)(2,1)}, u32[]{:S(2)}) copy-start(bf16[384,384]{1,0:T(8,128)(2,1)} %constant.24.clone.w_fine) | copy-start | bytes 884740
  7.9 0.9 %copy-start.6 = (f32[2,3,16,512]{3,2,1,0:T(8,128)S(1)}, f32[2,3,16,512]{3,2,1,0:T(8,128)}, u32[]{:S(2)}) copy-start(f32[2,3,16,512]{3,2,1,0:T(8,128)} %past.1) | copy-start | bytes 589828
  8.8 0.9 %copy-start.7 = (bf16[768,128]{1,0:T(8,128)(2,1)S(1)}, bf16[768,128]{1,0:T(8,128)(2,1)}, u32[]{:S(2)}) copy-start(bf16[768,128]{1,0:T(8,128)(2,1)} %constant.23.clone.w_pair_t) | copy-start | bytes 589828
  9.8 0.9 %copy-start.8 = (bf16[384,256]{1,0:T(8,128)(2,1)S(1)}, bf16[384,256]{1,0:T(8,128)(2,1)}, u32[]{:S(2)}) copy-start(bf16[384,256]{1,0:T(8,128)(2,1)} %constant.22.clone.w_pair) | copy-start | bytes 589828
  10.7 0.9 %copy-start.9 = (f32[96,384]{1,0:T(8,128)S(1)}, f32[96,384]{1,0:T(8,128)}, u32[]{:S(2)}) copy-start(f32[96,384]{1,0:T(8,128)} %constant.31.clone.fine_mass) | copy-start | bytes 442372
  11.6 0.9 %copy-start.10 = (f32[208,128]{1,0:T(8,128)S(1)}, f32[208,128]{1,0:T(8,128)}, u32[]{:S(2)}) copy-start(f32[208,128]{1,0:T(8,128)} %constant.29.clone.coef) | copy-start | bytes 319492
  12.5 0.9 %copy-start.11 = (f32[3,16,512]{2,1,0:T(8,128)S(1)}, f32[3,16,512]{2,1,0:T(8,128)}, u32[]{:S(2)}) copy-start(f32[3,16,512]{2,1,0:T(8,128)} %metric.1) | copy-start | bytes 294916
  13.4 0.8 %copy-start.12 = (f32[2,64,128]{2,1,0:T(8,128)S(1)}, f32[2,64,128]{2,1,0:T(8,128)}, u32[]{:S(2)}) copy-start(f32[2,64,128]{2,1,0:T(8,128)} %constant.30.clone.nodes) | copy-start | bytes 196612
  14.2 0.8 %copy-start.13 = (f32[16,512]{1,0:T(8,128)S(1)}, f32[16,512]{1,0:T(8,128)}, u32[]{:S(2)}) copy-start(f32[16,512]{1,0:T(8,128)} %jacobian.1) | copy-start | bytes 98308
where the time goes:
time: 65.3 us; the launch traced here: 64.6 us
  Pallas kernels  48.4 us (74%)
  local copies, waits for them, and re-layouts  15.6 us (24%)
    pallas_call x1, Pallas kernels, shards(): pl.pallas_call(functools.partial(kernel, count), out_shape=(block, block)...  48.4 us
    unnamed x32, local copies, waits for them, and re-layouts  14.8 us

commit v1 on v0

--- a/solution.py
+++ b/solution.py
@@ -138,7 +138,8 @@
     exact = np.asarray(matrix, np.float32)
     high = exact.astype(jnp.bfloat16)
     low = (exact - high.astype(np.float32)).astype(jnp.bfloat16)
-    return np.concatenate([high, high, low], axis=0)
+    columns = range(0, exact.shape[1], LANES)
+    return np.concatenate([part[:, c : c + LANES] for c in columns for part in (high, low)])
 
 
 def halves(matrix):
@@ -216,29 +217,37 @@
     eigen = np.zeros((2, LANES))
     eigen[0, :100] = t["eigen_around"]
     eigen[1, :100] = t["eigen_radial"]
-    share = np.ones((NP, NP, NP))
-    share[0] *= 0.5
-    share[-1] *= 0.5
-    share[:, 0] *= 0.5
-    share[:, -1] *= 0.5
-    nodes = np.stack([by_tile(t["mass_three"]), by_tile(share)])
-    arrays = [
-        split_rows(pair),
-        split_rows(pair.T),
-        split_rows(fine),
-        split_rows(fine_slope),
-        split_rows(fine.T),
-        split_rows(ahead),
-        split_rows(back.T),
-        np.concatenate([halves(d), halves(d.T), halves(itp), halves(slope), halves(itp.T)]),
-        nodes,
-        np.asarray(np.repeat(fine_mass, ES, axis=0), np.float32),
-        np.asarray(eigen, np.float32),
-    ]
-    return arrays, np.asarray(s, np.float32), np.asarray(t["eigen_axial"], np.float32)
-
-
+    nodes = by_tile(t["mass_three"])
+    weights = np.concatenate(
+        [split_rows(m) for m in (pair, pair.T, fine, fine_slope, fine.T, ahead, back.T)]
+    )
+    along = np.concatenate([halves(d), halves(d.T), halves(itp), halves(slope), halves(itp.T)])
+    fine_mass = np.repeat(fine_mass, ES, axis=0)
+    tables = np.concatenate(
+        [along, nodes]
+        + [fine_mass[:, c : c + LANES] for c in range(0, 384, LANES)]
+        + [np.pad(eigen, ((0, 6), (0, 0)))]
+    )
+    return (
+        weights,
+        np.asarray(tables, np.float32),
+        np.asarray(s, np.float32),
+        np.asarray(t["eigen_axial"], np.float32),
+    )
+
+
+PAIR = (0, 128, 256)
+PAIR_T = (512, 256, 128)
+FINE = (1024, 128, 384)
+SLOPE = (1792, 128, 768)
+FINE_T = (3328, 384, 128)
+AHEAD = (4096, 256, 256)
+BACK = (5120, 256, 256)
+TABLE_NODES, TABLE_FINE, TABLE_EIGEN = 208, 272, 560
 COEF_D, COEF_DT, COEF_I, COEF_S, COEF_IT = 0, 32, 64, 112, 160
+
+
+OPERANDS = 7
 
 
 def stages_of(count):
@@ -255,24 +264,13 @@
 
 def kernel(
     count,
-    velocity,
-    past,
-    metric,
-    jacobian,
-    slots,
-    w_pair,
-    w_pair_t,
-    w_fine,
-    w_slope,
-    w_fine_t,
-    w_ahead,
-    w_back,
-    coef,
-    nodes,
-    fine_mass,
-    eigen,
-    pressure_ref,
-    residual_ref,
+    *refs,
+):
+    operands, refs = refs[:OPERANDS], refs[OPERANDS:]
+    pressure_ref, residual_ref = refs[:2]
+    held, refs = refs[2 : 2 + OPERANDS], refs[2 + OPERANDS :]
+    (
+        load_sem,
     send_left,
     send_right,
     from_left,
@@ -285,8 +283,22 @@
     from_right_sem,
     gather_send_sem,
     gather_recv_sem,
-):
-    _, solve, eigen_axial = constants()
+    ) = refs
+    split = [(0, None)] * 5 + [(0, AHEAD[0]), (AHEAD[0], None), (0, None)]
+    loads = []
+    for i, (at, end) in enumerate(split):
+        which = min(i, 5) if i < 7 else 6
+        rows = slice(None) if i < 5 else pl.ds(at, (end or operands[which].shape[0]) - at)
+        loads.append(
+            pltpu.make_async_copy(
+                operands[which].at[rows], held[which].at[rows], load_sem.at[i]
+            )
+        )
+    for i in (3, 2, 0, 7, 5, 1, 4, 6):
+        loads[i].start()
+    velocity, past, metric, jacobian, slots, weights, tables = held
+
+    _, _, solve, eigen_axial = constants()
     me = lax.axis_index("dom")
     left = lax.rem(me + count - 1, count)
     right = lax.rem(me + 1, count)
@@ -320,8 +332,16 @@
     def mm(x, w):
         high = x.astype(jnp.bfloat16)
         rest = (x - high.astype(jnp.float32)).astype(jnp.bfloat16)
+        at, depth, width = w
+        columns = []
+        for c in range(width // LANES):
+            top = weights[at + 2 * c * depth : at + (2 * c + 1) * depth]
+            bottom = weights[at + (2 * c + 1) * depth : at + (2 * c + 2) * depth]
+            columns.append(jnp.concatenate([top, top, bottom], axis=0))
         return jnp.dot(
-            jnp.concatenate([high, rest, high], axis=1), w[...], preferred_element_type=jnp.float32
+            jnp.concatenate([high, rest, high], axis=1),
+            jnp.concatenate(columns, axis=1),
+            preferred_element_type=jnp.float32,
         )
 
     def swap(tile):
@@ -335,17 +355,17 @@
             acc = None
             for into in range(len(parts)):
                 at = base + 2 * (out * len(parts) + into)
-                term = coef[at : at + 1] * parts[into] + coef[at + 1 : at + 2] * swapped[into]
+                term = tables[at : at + 1] * parts[into] + tables[at + 1 : at + 2] * swapped[into]
                 acc = term if acc is None else acc + term
             results.append(acc)
         return stack(results)
 
     def gradient(field):
-        paired = mm(field, w_pair)
+        paired = mm(field, PAIR)
         return along(field, COEF_D, 4), paired[:, :LANES], paired[:, LANES:]
 
     def gradient_t(axial, around, radial):
-        paired = mm(jnp.concatenate([around, radial], axis=1), w_pair_t)
+        paired = mm(jnp.concatenate([around, radial], axis=1), PAIR_T)
         return paired + along(axial, COEF_DT, 4)
 
     def before(tile):
@@ -385,21 +405,26 @@
         )
         return rows, to_left, to_right
 
-    def exchange(step, for_left, for_right):
+    def send(step, for_left, for_right):
         rows, to_left, to_right = copies(step)
         send_left[rows] = for_left
         to_left.start()
         send_right[rows] = for_right
         to_right.start()
+
+    def receive(step):
+        rows, to_left, to_right = copies(step)
         to_right.wait_recv()
         to_left.wait_recv()
         return from_left[rows], from_right[rows]
 
+    def send_faces(step, fields):
+        parts = [tiles(field) for field in fields]
+        send(step, stack([p[0] for p in parts]), stack([p[3] for p in parts]))
+
     def axial_sum(step, fields):
         parts = [tiles(field) for field in fields]
-        lefts, rights = exchange(
-            step, stack([p[0] for p in parts]), stack([p[3] for p in parts])
-        )
+        lefts, rights = receive(step)
         lefts, rights = tiles(lefts), tiles(rights)
         results = []
         for p, far_left, far_right in zip(parts, lefts, rights):
@@ -418,7 +443,13 @@
     def element_field(ref, *index):
         return stack([ref[index + (slice(None), pl.ds(j * LANES, LANES))] for j in range(4)])
 
-    weight3, share = nodes[0], nodes[1]
+    for i in (3, 2, 0, 7, 5, 1, 4):
+        loads[i].wait()
+    weight3 = tables[TABLE_NODES:TABLE_FINE]
+    fine_mass = jnp.concatenate(
+        [tables[TABLE_FINE + 96 * c : TABLE_FINE + 96 * (c + 1)] for c in range(3)], axis=1
+    )
+    eigen = tables[TABLE_EIGEN:]
     jac = element_field(jacobian)
     mass = jac * weight3
     metrics = [element_field(metric, d) for d in range(3)]
@@ -427,10 +458,10 @@
     coarse = [along(jac, COEF_I, 6)]
     coarse += [along(newest[d] * metrics[d], COEF_I, 6) for d in range(3)]
     coarse += [along(newest[i], COEF_S, 6) for i in range(3)]
-    fine = mm(stack(coarse), w_fine)
+    fine = mm(stack(coarse), FINE)
     fine = [fine[i * 96 : (i + 1) * 96] for i in range(7)]
-    crossed = mm(stack([along(newest[i], COEF_I, 6) for i in range(3)]), w_slope)
-    fine_jac = fine[0] * fine_mass[...]
+    crossed = mm(stack([along(newest[i], COEF_I, 6) for i in range(3)]), SLOPE)
+    fine_jac = fine[0] * fine_mass
     products = []
     for i in range(3):
         rows = slice(i * 96, (i + 1) * 96)
@@ -442,12 +473,12 @@
                 + fine[3] * crossed[rows, 384:]
             )
         )
-    advected = mm(stack(products), w_fine_t)
+    advected = mm(stack(products), FINE_T)
     guessed = [
         3.0 * newest[i] - 3.0 * element_field(velocity, 1, i) + element_field(velocity, 2, i)
         for i in range(3)
     ]
-    paired = mm(stack(guessed), w_pair)
+    paired = mm(stack(guessed), PAIR)
     slopes = jnp.concatenate(
         [
             stack([squares[1] * paired[i * 64 : (i + 1) * 64, :LANES] for i in range(3)]),
@@ -455,7 +486,7 @@
         ],
         axis=1,
     )
-    paired_t = mm(slopes, w_pair_t)
+    paired_t = mm(slopes, PAIR_T)
     forcing = []
     for i in range(3):
         convect = along(advected[i * 96 : (i + 1) * 96], COEF_IT, 4)
@@ -479,14 +510,18 @@
     rest = wide - first.astype(jnp.float32)
     second = rest.astype(jnp.bfloat16)
     third = (rest - second.astype(jnp.float32)).astype(jnp.bfloat16)
-    position = lax.broadcasted_iota(jnp.int32, (ES, 3 * ES), 0)
-    chosen = jnp.where(slots[...] == position, 1.0, 0.0).astype(jnp.bfloat16)
+    position = lax.broadcasted_iota(jnp.int32, (ES, ES), 0)
+    chosen = jnp.where(slots[...] == position, 1.0, 0.0)
+    chosen = jnp.concatenate([chosen, chosen, chosen], axis=1).astype(jnp.bfloat16)
     placed = jnp.dot(chosen, stack([first, second, third]), preferred_element_type=jnp.float32)
     fields = [
         stack([placed[:, (4 * f + j) * LANES : (4 * f + j + 1) * LANES] for j in range(4)])
         for f in range(7)
     ]
     forcing, mass, metrics = fields[:3], fields[3], fields[4:]
+    around = [around_sum(f) for f in forcing + [mass]]
+    pl.semaphore_wait(barrier, len(greeted))
+    send_faces(0, around)
     lumps = [mass * m for m in metrics]
     squares = [lumps[d] * metrics[d] for d in range(3)]
 
@@ -500,11 +535,13 @@
     )
     inverse = [1.0 / (scales[0] * float(eigen_axial[k]) + flat) for k in range(10)]
 
-    pl.semaphore_wait(barrier, len(greeted))
-    summed, _ = axial_sum(0, [around_sum(f) for f in forcing + [mass]])
+    summed, _ = axial_sum(0, around)
     accel = [lumps[d] * (summed[d] / summed[3]) for d in range(3)]
-    divergence = around_sum(gradient_t(accel[0], accel[1], accel[2]))
-    (source,), source_halo = axial_sum(1, [divergence])
+    divergence = gradient_t(accel[0], accel[1], accel[2])
+    source = around_sum(divergence)
+    send_faces(1, [source])
+    loads[6].wait()
+    (source,), source_halo = axial_sum(1, [source])
 
     def smooth(step, field, halo):
         parts = tiles(field) + [halo]
@@ -512,7 +549,7 @@
             jnp.where(node_s == 6, before(p), jnp.where(node_s == 1, after(p), 0.0))
             for p in parts
         ]
-        modes = mm(jnp.concatenate([stack(parts), stack(sides)], axis=1), w_ahead)
+        modes = mm(jnp.concatenate([stack(parts), stack(sides)], axis=1), AHEAD)
         rows = tiles(modes)
         order = [rows[4][:, :LANES]]
         for j in range(4):
@@ -532,40 +569,50 @@
             restored.append(acc)
         lows = [restored[1], restored[3], restored[5], restored[7], restored[0]]
         highs = [restored[2], restored[4], restored[6], restored[8], restored[9]]
-        given = mm(jnp.concatenate([stack(lows), stack(highs)], axis=1), w_back)
+        given = mm(jnp.concatenate([stack(lows), stack(highs)], axis=1), BACK)
         own, other = tiles(given[:, :LANES]), tiles(given[:, LANES:])
         own = [
             o + jnp.where(node_s <= 1, before(n), jnp.where(node_s >= 6, after(n), 0.0))
             for o, n in zip(own, other)
         ]
-        far_left, far_right = exchange(
+        send(
             step,
             jnp.where(low, own[4], swap(own[0])),
             jnp.where(low, swap(own[3]), own[4]),
         )
+        far_left, far_right = receive(step)
         return stack([own[0] + far_left, own[1], own[2], own[3] + far_right])
 
-    def apply(step, field):
+    def apply(field):
         axial, around, radial = gradient(field)
         local = gradient_t(squares[0] * axial, squares[1] * around, squares[2] * radial)
-        local = around_sum(local + mass_shift * mass * field)
-        (image,), halo = axial_sum(step, [local])
-        return image, halo
+        return local + mass_shift * mass * field
 
     def inner(one, two):
-        return jnp.sum(one * two * share, axis=0, keepdims=True)
-
-    spaces, images = [], []
+        return jnp.sum(one * two, axis=0, keepdims=True)
+
+    spaces, images, dots = [], [], {}
     current, halo = source, source_halo
     for it in range(ITERS):
-        spaces.append(smooth(2 + 2 * it, current, halo))
-        current, halo = apply(3 + 2 * it, spaces[-1])
-        images.append(current)
-
-    pairs = [(source, spaces[0])] + [
-        (images[i], spaces[j]) for i in range(3) for j in range(i, 3)
-    ]
-    value = jnp.concatenate([inner(x, y) for x, y in pairs] + [jnp.zeros((1, LANES))], axis=0)
+        step = 3 + 2 * it
+        spaces.append(smooth(step - 1, current, halo))
+        local = apply(spaces[-1])
+        image = around_sum(local)
+        send_faces(step, [image])
+        if it == 0:
+            head = inner(divergence, spaces[0])
+        for j in range(it + 1):
+            dots[j, it] = inner(local, spaces[j])
+        if it < ITERS - 1:
+            (current,), halo = axial_sum(step, [image])
+            images.append(current)
+
+    value = jnp.concatenate(
+        [head]
+        + [dots[i, j] for i in range(3) for j in range(i, 3)]
+        + [jnp.zeros((1, LANES), jnp.float32)],
+        axis=0,
+    )
     started = []
     for stage, (stride, size) in enumerate(stages):
         digit = lax.rem(me // stride, size)
@@ -630,6 +677,8 @@
             result[k] = step if result[k] is None else result[k] + step
             taken[k] = -step if taken[k] is None else taken[k] - step
         previous = rho
+    (current,), _ = axial_sum(ROUNDS - 1, [image])
+    images.append(current)
     final = [spaces[0] * result[0], source]
     for k in range(3):
         final[1] = final[1] + images[k] * taken[k]
@@ -653,18 +702,22 @@
 
 
 def shards(count, velocity, conv_past, metric, jacobian, element_slot):
-    arrays, _, _ = constants()
+    weights, tables, _, _ = constants()
     stages = stages_of(count)
     block = jax.ShapeDtypeStruct((A0, A1 * A2), jnp.float32)
     whole = pl.BlockSpec(memory_space=pltpu.VMEM)
     rows = (3 + ROUNDS) * ES
-    slots = jnp.tile(element_slot, 3).reshape(1, 3 * ES)
+    slots = element_slot.reshape(1, ES)
+    operands = [velocity, conv_past, metric, jacobian, slots]
+    operands += [jnp.asarray(weights), jnp.asarray(tables)]
     return pl.pallas_call(
         functools.partial(kernel, count),
         out_shape=(block, block),
-        in_specs=[whole] * (5 + len(arrays)),
+        in_specs=[pl.BlockSpec(memory_space=pltpu.HBM)] * len(operands),
         out_specs=(whole, whole),
-        scratch_shapes=[
+        scratch_shapes=[pltpu.VMEM(x.shape, x.dtype) for x in operands]
+        + [
+            pltpu.SemaphoreType.DMA((len(operands) + 1,)),
             pltpu.VMEM((rows, LANES), jnp.float32),
             pltpu.VMEM((rows, LANES), jnp.float32),
             pltpu.VMEM((rows, LANES), jnp.float32),
@@ -679,9 +732,9 @@
             pltpu.SemaphoreType.DMA((len(stages), 8)),
         ],
         compiler_params=pltpu.CompilerParams(
-            collective_id=0, has_side_effects=True, vmem_limit_bytes=40 * 1024 * 1024
+            collective_id=0, has_side_effects=True, vmem_limit_bytes=56 * 1024 * 1024
         ),
-    )(velocity, conv_past, metric, jacobian, slots, *[jnp.asarray(a) for a in arrays])
+    )(*operands)
 
 
 def solution(mesh):

time: 65.3 us -> 49.5 us (0.76)
  local copies, waits for them, and re-layouts: 15.6 us -> 2.72 us
  Pallas kernels: 48.4 us -> 45.9 us
    unnamed x32 -> x2, local copies, waits for them, and re-layouts: 14.8 us -> 2.72 us
    pallas_call x1, Pallas kernels: 48.4 us -> 45.9 us  [shards(): pl.pallas_call(functools.partial(kernel, count), out_shape=(block, block)...]
    another operation x2 -> x0, local copies, waits for them, and re-layouts: 0.74 us -> none  [shards(): slots = jnp.tile(element_slot, 3).reshape(1, 3 * ES)]
where the time goes in v1:
time: 49.5 us; the launch traced here: 49.2 us
  Pallas kernels  45.9 us (93%)
  local copies, waits for them, and re-layouts  2.72 us (5%)
  between operations  0.64 us (1%)
    pallas_call x1, Pallas kernels, shards(): pl.pallas_call(functools.partial(kernel, count), out_shape=(block, block)...  45.9 us
    unnamed x2, local copies, waits for them, and re-layouts  2.72 us

profile of v1, /device:TPU:0, one launch (start us, length us, event | category | flops | bytes accessed | tf_op | source)
XLA Modules:
  0.0 49.2 jit_solution(7313081213157761611)
XLA Ops:
  0.6 45.9 %shard_map.86 = (f32[8,896]{1,0:T(8,128)}, f32[8,896]{1,0:T(8,128)}) custom-call(f32[3,3,16,512]{3,2,1,0:T(8,128)} %refs_0_.1, f32[2,3,16,512]{3,2,1,0:T(8,128)} %refs_1_.1, f32[3,16,512]{2,1,0:T(8,128)} %refs_2_.1, f32[16,512]{1,0:T(8,128)} %refs_3_.1, s32[1,16]{1,0:T(1,128)} %bitcast.1, bf16[6144,128]{1,0:T(8,128)(2,1)} %constant.4.clone.refs_5_, ...), custom_call_target="tpu_custom_call" | custom-call | tf_op jit(solution)/shard_map/pallas_call | solution.py:713
  46.5 1.4 %copy.11 = f32[8,896]{1,0:T(8,128)} copy(f32[8,896]{1,0:T(8,128)} %get-tuple-element.4) | data formatting | bytes 57344
  47.9 1.4 %copy.12 = f32[8,896]{1,0:T(8,128)} copy(f32[8,896]{1,0:T(8,128)} %get-tuple-element.5) | data formatting | bytes 57344

commit v2 on v1

--- a/solution.py
+++ b/solution.py
@@ -15,7 +15,8 @@
 A0 = 8
 A1 = 112
 A2 = 8
-ROUNDS = 8
+ROUNDS = 5
+WAYS = 4
 LANES = 128
 MESH = pl.DeviceIdType.MESH
 
@@ -271,18 +272,17 @@
     held, refs = refs[2 : 2 + OPERANDS], refs[2 + OPERANDS :]
     (
         load_sem,
-    send_left,
-    send_right,
-    from_left,
-    from_right,
-    gathered,
-    turned,
-    send_left_sem,
-    send_right_sem,
-    from_left_sem,
-    from_right_sem,
-    gather_send_sem,
-    gather_recv_sem,
+        first_out,
+        first_in,
+        outbox,
+        inbox,
+        inbox_far,
+        gathered,
+        turned,
+        send_sem,
+        recv_sem,
+        gather_send_sem,
+        gather_recv_sem,
     ) = refs
     split = [(0, None)] * 5 + [(0, AHEAD[0]), (AHEAD[0], None), (0, None)]
     loads = []
@@ -302,6 +302,8 @@
     me = lax.axis_index("dom")
     left = lax.rem(me + count - 1, count)
     right = lax.rem(me + 1, count)
+    far_left = lax.rem(me + count - 2, count)
+    far_right = lax.rem(me + 2, count)
     stages = stages_of(count)
 
     def peer(stage, offset):
@@ -311,7 +313,7 @@
         return me + (other - digit) * stride
 
     barrier = pltpu.get_barrier_semaphore()
-    greeted = [left, right] + [
+    greeted = [left, right, far_left, far_right] + [
         peer(stage, offset)
         for stage in range(len(stages))
         for offset in range(1, stages[stage][1])
@@ -385,60 +387,58 @@
         return stack(results)
 
     def copies(step):
-        at, size = (0, 4 * ES) if step == 0 else ((3 + step) * ES, ES)
-        rows = pl.ds(at, size)
-        to_left = pltpu.make_async_remote_copy(
-            src_ref=send_left.at[rows],
-            dst_ref=from_right.at[rows],
-            send_sem=send_left_sem.at[step],
-            recv_sem=from_right_sem.at[step],
-            device_id=(left,),
-            device_id_type=MESH,
+        if step == 0:
+            plan = [(first_out.at[0], first_in.at[1], left), (first_out.at[1], first_in.at[0], right)]
+        elif step < ROUNDS - 1:
+            plan = [
+                (outbox.at[step, pl.ds(0, ES)], inbox_far.at[step, 1], far_left),
+                (outbox.at[step, pl.ds(3 * ES, ES)], inbox_far.at[step, 0], far_right),
+                (outbox.at[step], inbox.at[step, 1], left),
+                (outbox.at[step], inbox.at[step, 0], right),
+            ]
+        else:
+            plan = [
+                (outbox.at[step, pl.ds(0, ES)], inbox_far.at[step, 1], left),
+                (outbox.at[step, pl.ds(3 * ES, ES)], inbox_far.at[step, 0], right),
+            ]
+        return [
+            pltpu.make_async_remote_copy(
+                src_ref=source,
+                dst_ref=target,
+                send_sem=send_sem.at[step, way],
+                recv_sem=recv_sem.at[step, way],
+                device_id=(other,),
+                device_id_type=MESH,
+            )
+            for way, (source, target, other) in enumerate(plan)
+        ]
+
+    def send(step, field):
+        outbox[step] = field
+        for copy in copies(step):
+            copy.start()
+
+    def receive(step):
+        for copy in copies(step):
+            copy.wait_recv()
+
+    def axial_sum(field, before_it, after_it):
+        parts = tiles(field)
+        return stack(
+            [
+                parts[0] + jnp.where(low, swap(before_it), 0.0),
+                parts[1],
+                parts[2],
+                parts[3] + jnp.where(low, 0.0, swap(after_it)),
+            ]
         )
-        to_right = pltpu.make_async_remote_copy(
-            src_ref=send_right.at[rows],
-            dst_ref=from_left.at[rows],
-            send_sem=send_right_sem.at[step],
-            recv_sem=from_left_sem.at[step],
-            device_id=(right,),
-            device_id_type=MESH,
-        )
-        return rows, to_left, to_right
-
-    def send(step, for_left, for_right):
-        rows, to_left, to_right = copies(step)
-        send_left[rows] = for_left
-        to_left.start()
-        send_right[rows] = for_right
-        to_right.start()
-
-    def receive(step):
-        rows, to_left, to_right = copies(step)
-        to_right.wait_recv()
-        to_left.wait_recv()
-        return from_left[rows], from_right[rows]
-
-    def send_faces(step, fields):
-        parts = [tiles(field) for field in fields]
-        send(step, stack([p[0] for p in parts]), stack([p[3] for p in parts]))
-
-    def axial_sum(step, fields):
-        parts = [tiles(field) for field in fields]
-        lefts, rights = receive(step)
-        lefts, rights = tiles(lefts), tiles(rights)
-        results = []
-        for p, far_left, far_right in zip(parts, lefts, rights):
-            results.append(
-                stack(
-                    [
-                        p[0] + jnp.where(low, swap(far_left), 0.0),
-                        p[1],
-                        p[2],
-                        p[3] + jnp.where(low, 0.0, swap(far_right)),
-                    ]
-                )
-            )
-        return results, jnp.where(low, lefts[0], rights[0])
+
+    def surrounded(step, field):
+        receive(step)
+        beside = [inbox[step, 0], inbox[step, 1]]
+        ends = [inbox_far[step, 0], inbox_far[step, 1]]
+        own = axial_sum(field, beside[0][3 * ES :], beside[1][:ES])
+        return own, beside, ends
 
     def element_field(ref, *index):
         return stack([ref[index + (slice(None), pl.ds(j * LANES, LANES))] for j in range(4)])
@@ -519,9 +519,6 @@
         for f in range(7)
     ]
     forcing, mass, metrics = fields[:3], fields[3], fields[4:]
-    around = [around_sum(f) for f in forcing + [mass]]
-    pl.semaphore_wait(barrier, len(greeted))
-    send_faces(0, around)
     lumps = [mass * m for m in metrics]
     squares = [lumps[d] * metrics[d] for d in range(3)]
 
@@ -529,59 +526,67 @@
         parts = tiles(field)
         return jnp.sum(parts[0] + parts[1] + parts[2] + parts[3], axis=1, keepdims=True) / 8.0
 
-    scales = [total(square) for square in squares]
     flat = (
-        scales[1] * eigen[0:1] + scales[2] * eigen[1:2] + mass_shift * total(mass)
-    )
-    inverse = [1.0 / (scales[0] * float(eigen_axial[k]) + flat) for k in range(10)]
-
-    summed, _ = axial_sum(0, around)
+        total(squares[1]) * eigen[0:1]
+        + total(squares[2]) * eigen[1:2]
+        + mass_shift * total(mass)
+    )
+    steep = jnp.broadcast_to(total(squares[0]), (ES, LANES))
+
+    around = [around_sum(f) for f in forcing + [mass]]
+    first_out[0] = stack([f[:ES] for f in around] + [flat, steep])
+    first_out[1] = stack([f[3 * ES :] for f in around] + [flat, steep])
+    pl.semaphore_wait(barrier, len(greeted))
+    for copy in copies(0):
+        copy.start()
+    receive(0)
+    lefts, rights = tiles(first_in[0]), tiles(first_in[1])
+    summed = [axial_sum(around[f], lefts[f], rights[f]) for f in range(4)]
     accel = [lumps[d] * (summed[d] / summed[3]) for d in range(3)]
     divergence = gradient_t(accel[0], accel[1], accel[2])
     source = around_sum(divergence)
-    send_faces(1, [source])
+    send(1, source)
     loads[6].wait()
-    (source,), source_halo = axial_sum(1, [source])
-
-    def smooth(step, field, halo):
-        parts = tiles(field) + [halo]
+    flats = stack([lefts[4], flat, rights[4]])
+    steeps = stack([lefts[5], steep, rights[5]])
+    inverse = [1.0 / (steeps * float(eigen_axial[k]) + flats) for k in range(10)]
+    source, beside, ends = surrounded(1, source)
+
+    def combine(weight, parts):
+        acc = parts[0] * float(weight[0])
+        for one, part in zip(weight[1:], parts[1:]):
+            acc = acc + part * float(one)
+        return acc
+
+    def smooth(own, beside, ends):
+        lower, upper = tiles(beside[0]), tiles(beside[1])
+        lower[0] = lower[0] + jnp.where(low, swap(ends[0]), 0.0)
+        upper[3] = upper[3] + jnp.where(low, 0.0, swap(ends[1]))
+        parts = [jnp.where(low, ends[0], ends[1])] + lower + upper + tiles(own)
         sides = [
             jnp.where(node_s == 6, before(p), jnp.where(node_s == 1, after(p), 0.0))
             for p in parts
         ]
-        modes = mm(jnp.concatenate([stack(parts), stack(sides)], axis=1), AHEAD)
-        rows = tiles(modes)
-        order = [rows[4][:, :LANES]]
-        for j in range(4):
-            order += [rows[j][:, :LANES], rows[j][:, LANES:]]
-        order.append(rows[4][:, LANES:])
-        spectra = []
-        for k in range(10):
-            acc = order[0] * float(solve[0, k])
-            for a in range(1, 10):
-                acc = acc + order[a] * float(solve[a, k])
-            spectra.append(acc * inverse[k])
-        restored = []
-        for a in range(10):
-            acc = spectra[0] * float(solve[a, 0])
-            for k in range(1, 10):
-                acc = acc + spectra[k] * float(solve[a, k])
-            restored.append(acc)
-        lows = [restored[1], restored[3], restored[5], restored[7], restored[0]]
-        highs = [restored[2], restored[4], restored[6], restored[8], restored[9]]
-        given = mm(jnp.concatenate([stack(lows), stack(highs)], axis=1), BACK)
-        own, other = tiles(given[:, :LANES]), tiles(given[:, LANES:])
-        own = [
-            o + jnp.where(node_s <= 1, before(n), jnp.where(node_s >= 6, after(n), 0.0))
-            for o, n in zip(own, other)
-        ]
-        send(
-            step,
-            jnp.where(low, own[4], swap(own[0])),
-            jnp.where(low, swap(own[3]), own[4]),
+        modes = tiles(mm(jnp.concatenate([stack(parts), stack(sides)], axis=1), AHEAD))
+        firsts = [-7, -5, -3, -1, 7, 9, 11, 13, 0, 2, 4, 6]
+        grid = {-8: modes[0][:, :LANES], 15: modes[0][:, LANES:]}
+        for row, mode in zip(firsts, modes[1:]):
+            grid[row], grid[row + 1] = mode[:, :LANES], mode[:, LANES:]
+        order = [stack([grid[a - 7], grid[a], grid[a + 7]]) for a in range(-1, 9)]
+        spectra = [combine(solve[:, k], order) * inverse[k] for k in range(10)]
+        slabs = [[spectrum[b * ES : (b + 1) * ES] for spectrum in spectra] for b in range(3)]
+        rows = [combine(solve[a + 1], slabs[1]) for a in range(NP)]
+        rows[0] = rows[0] + combine(solve[8], slabs[0])
+        rows[1] = rows[1] + combine(solve[9], slabs[0])
+        rows[6] = rows[6] + combine(solve[0], slabs[2])
+        rows[7] = rows[7] + combine(solve[1], slabs[2])
+        given = mm(jnp.concatenate([stack(rows[0::2]), stack(rows[1::2])], axis=1), BACK)
+        return stack(
+            [
+                o + jnp.where(node_s <= 1, before(n), jnp.where(node_s >= 6, after(n), 0.0))
+                for o, n in zip(tiles(given[:, :LANES]), tiles(given[:, LANES:]))
+            ]
         )
-        far_left, far_right = receive(step)
-        return stack([own[0] + far_left, own[1], own[2], own[3] + far_right])
 
     def apply(field):
         axial, around, radial = gradient(field)
@@ -592,19 +597,18 @@
         return jnp.sum(one * two, axis=0, keepdims=True)
 
     spaces, images, dots = [], [], {}
-    current, halo = source, source_halo
+    current = source
     for it in range(ITERS):
-        step = 3 + 2 * it
-        spaces.append(smooth(step - 1, current, halo))
+        spaces.append(smooth(current, beside, ends))
         local = apply(spaces[-1])
         image = around_sum(local)
-        send_faces(step, [image])
+        send(2 + it, image)
         if it == 0:
             head = inner(divergence, spaces[0])
         for j in range(it + 1):
             dots[j, it] = inner(local, spaces[j])
         if it < ITERS - 1:
-            (current,), halo = axial_sum(step, [image])
+            current, beside, ends = surrounded(2 + it, image)
             images.append(current)
 
     value = jnp.concatenate(
@@ -677,8 +681,8 @@
             result[k] = step if result[k] is None else result[k] + step
             taken[k] = -step if taken[k] is None else taken[k] - step
         previous = rho
-    (current,), _ = axial_sum(ROUNDS - 1, [image])
-    images.append(current)
+    receive(ROUNDS - 1)
+    images.append(axial_sum(image, inbox_far[ROUNDS - 1, 0], inbox_far[ROUNDS - 1, 1]))
     final = [spaces[0] * result[0], source]
     for k in range(3):
         final[1] = final[1] + images[k] * taken[k]
@@ -694,9 +698,8 @@
             ref[:, p * 56 : (p + 1) * 56] = block[:, :56]
 
     for step in range(ROUNDS):
-        _, to_left, to_right = copies(step)
-        to_left.wait_send()
-        to_right.wait_send()
+        for copy in copies(step):
+            copy.wait_send()
     for copy in started:
         copy.wait_send()
 
@@ -706,7 +709,6 @@
     stages = stages_of(count)
     block = jax.ShapeDtypeStruct((A0, A1 * A2), jnp.float32)
     whole = pl.BlockSpec(memory_space=pltpu.VMEM)
-    rows = (3 + ROUNDS) * ES
     slots = element_slot.reshape(1, ES)
     operands = [velocity, conv_past, metric, jacobian, slots]
     operands += [jnp.asarray(weights), jnp.asarray(tables)]
@@ -718,16 +720,15 @@
         scratch_shapes=[pltpu.VMEM(x.shape, x.dtype) for x in operands]
         + [
             pltpu.SemaphoreType.DMA((len(operands) + 1,)),
-            pltpu.VMEM((rows, LANES), jnp.float32),
-            pltpu.VMEM((rows, LANES), jnp.float32),
-            pltpu.VMEM((rows, LANES), jnp.float32),
-            pltpu.VMEM((rows, LANES), jnp.float32),
+            pltpu.VMEM((2, 6 * ES, LANES), jnp.float32),
+            pltpu.VMEM((2, 6 * ES, LANES), jnp.float32),
+            pltpu.VMEM((ROUNDS, 4 * ES, LANES), jnp.float32),
+            pltpu.VMEM((ROUNDS, 2, 4 * ES, LANES), jnp.float32),
+            pltpu.VMEM((ROUNDS, 2, ES, LANES), jnp.float32),
             pltpu.VMEM((len(stages), 8, 8, LANES), jnp.float32),
             pltpu.VMEM((2, NP * ES, LANES), jnp.float32),
-            pltpu.SemaphoreType.DMA((ROUNDS,)),
-            pltpu.SemaphoreType.DMA((ROUNDS,)),
-            pltpu.SemaphoreType.DMA((ROUNDS,)),
-            pltpu.SemaphoreType.DMA((ROUNDS,)),
+            pltpu.SemaphoreType.DMA((ROUNDS, WAYS)),
+            pltpu.SemaphoreType.DMA((ROUNDS, WAYS)),
             pltpu.SemaphoreType.DMA((len(stages), 8)),
             pltpu.SemaphoreType.DMA((len(stages), 8)),
         ],

time: 49.5 us -> 40.2 us (0.81)
  Pallas kernels: 45.9 us -> 36.6 us
    pallas_call x1, Pallas kernels: 45.9 us -> 36.6 us  [shards(): pl.pallas_call(functools.partial(kernel, count), out_shape=(block, block)...]
where the time goes in v2:
time: 40.2 us; the launch traced here: 39.9 us
  Pallas kernels  36.6 us (91%)
  local copies, waits for them, and re-layouts  2.72 us (7%)
  between operations  0.64 us (2%)
    pallas_call x1, Pallas kernels, shards(): pl.pallas_call(functools.partial(kernel, count), out_shape=(block, block)...  36.6 us
    unnamed x2, local copies, waits for them, and re-layouts  2.72 us

profile of v2, /device:TPU:0, one launch (start us, length us, event | category | flops | bytes accessed | tf_op | source)
XLA Modules:
  0.0 39.9 jit_solution(14495069494997789039)
XLA Ops:
  0.6 36.6 %shard_map.86 = (f32[8,896]{1,0:T(8,128)}, f32[8,896]{1,0:T(8,128)}) custom-call(f32[3,3,16,512]{3,2,1,0:T(8,128)} %refs_0_.1, f32[2,3,16,512]{3,2,1,0:T(8,128)} %refs_1_.1, f32[3,16,512]{2,1,0:T(8,128)} %refs_2_.1, f32[16,512]{1,0:T(8,128)} %refs_3_.1, s32[1,16]{1,0:T(1,128)} %bitcast.1, bf16[6144,128]{1,0:T(8,128)(2,1)} %constant.4.clone.refs_5_, ...), custom_call_target="tpu_custom_call" | custom-call | tf_op jit(solution)/shard_map/pallas_call | solution.py:715
  37.2 1.4 %copy.11 = f32[8,896]{1,0:T(8,128)} copy(f32[8,896]{1,0:T(8,128)} %get-tuple-element.4) | data formatting | bytes 57344
  38.6 1.4 %copy.12 = f32[8,896]{1,0:T(8,128)} copy(f32[8,896]{1,0:T(8,128)} %get-tuple-element.5) | data formatting | bytes 57344

commit v3 on v2

--- a/solution.py
+++ b/solution.py
@@ -17,6 +17,7 @@
 A2 = 8
 ROUNDS = 5
 WAYS = 4
+PEERS = 32
 LANES = 128
 MESH = pl.DeviceIdType.MESH
 
@@ -255,7 +256,7 @@
     stages = []
     stride = 1
     while stride < count:
-        size = min(8, count // stride)
+        size = min(PEERS, count // stride)
         while (count // stride) % size:
             size -= 1
         stages.append((stride, size))
@@ -279,6 +280,7 @@
         inbox_far,
         gathered,
         turned,
+        basis,
         send_sem,
         recv_sem,
         gather_send_sem,
@@ -443,8 +445,8 @@
     def element_field(ref, *index):
         return stack([ref[index + (slice(None), pl.ds(j * LANES, LANES))] for j in range(4)])
 
-    for i in (3, 2, 0, 7, 5, 1, 4):
-        loads[i].wait()
+    loads[7].wait()
+    loads[3].wait()
     weight3 = tables[TABLE_NODES:TABLE_FINE]
     fine_mass = jnp.concatenate(
         [tables[TABLE_FINE + 96 * c : TABLE_FINE + 96 * (c + 1)] for c in range(3)], axis=1
@@ -452,12 +454,15 @@
     eigen = tables[TABLE_EIGEN:]
     jac = element_field(jacobian)
     mass = jac * weight3
+    coarse = [along(jac, COEF_I, 6)]
+    loads[2].wait()
     metrics = [element_field(metric, d) for d in range(3)]
     squares = [mass * m * m for m in metrics]
+    loads[0].wait()
     newest = [element_field(velocity, 0, i) for i in range(3)]
-    coarse = [along(jac, COEF_I, 6)]
     coarse += [along(newest[d] * metrics[d], COEF_I, 6) for d in range(3)]
     coarse += [along(newest[i], COEF_S, 6) for i in range(3)]
+    loads[5].wait()
     fine = mm(stack(coarse), FINE)
     fine = [fine[i * 96 : (i + 1) * 96] for i in range(7)]
     crossed = mm(stack([along(newest[i], COEF_I, 6) for i in range(3)]), SLOPE)
@@ -488,6 +493,8 @@
     )
     paired_t = mm(slopes, PAIR_T)
     forcing = []
+    loads[1].wait()
+    loads[4].wait()
     for i in range(3):
         convect = along(advected[i * 96 : (i + 1) * 96], COEF_IT, 4)
         stiff = paired_t[i * 64 : (i + 1) * 64] + along(
@@ -596,6 +603,14 @@
     def inner(one, two):
         return jnp.sum(one * two, axis=0, keepdims=True)
 
+    def turn(which, field):
+        for j, tile in enumerate(tiles(field)):
+            turned[which, pl.ds(2 * j * ES, ES)] = tile
+            turned[which, pl.ds((2 * j + 1) * ES, ES)] = swap(tile)
+        for p in range(ES):
+            block = turned[which, pl.ds(p, NP, stride=ES), :]
+            basis[which, :, p * 56 : (p + 1) * 56] = block[:, :56]
+
     spaces, images, dots = [], [], {}
     current = source
     for it in range(ITERS):
@@ -608,6 +623,11 @@
         for j in range(it + 1):
             dots[j, it] = inner(local, spaces[j])
         if it < ITERS - 1:
+            turn(2 * it, spaces[it])
+            if it == 0:
+                turn(6, current)
+            else:
+                turn(2 * it - 1, current)
             current, beside, ends = surrounded(2 + it, image)
             images.append(current)
 
@@ -632,6 +652,12 @@
             )
             copy.start()
             started.append(copy)
+        if stage == 0:
+            turn(4, spaces[2])
+            turn(3, images[1])
+            receive(ROUNDS - 1)
+            ends = [inbox_far[ROUNDS - 1, 0], inbox_far[ROUNDS - 1, 1]]
+            turn(5, axial_sum(image, ends[0], ends[1]))
         for copy in started[1 - size :]:
             copy.wait_recv()
         value = gathered[stage, 0]
@@ -681,21 +707,8 @@
             result[k] = step if result[k] is None else result[k] + step
             taken[k] = -step if taken[k] is None else taken[k] - step
         previous = rho
-    receive(ROUNDS - 1)
-    images.append(axial_sum(image, inbox_far[ROUNDS - 1, 0], inbox_far[ROUNDS - 1, 1]))
-    final = [spaces[0] * result[0], source]
-    for k in range(3):
-        final[1] = final[1] + images[k] * taken[k]
-        if k:
-            final[0] = final[0] + spaces[k] * result[k]
-
-    for which, ref in enumerate((pressure_ref, residual_ref)):
-        for j, tile in enumerate(tiles(final[which])):
-            turned[which, pl.ds(2 * j * ES, ES)] = tile
-            turned[which, pl.ds((2 * j + 1) * ES, ES)] = swap(tile)
-        for p in range(ES):
-            block = turned[which, pl.ds(p, NP, stride=ES), :]
-            ref[:, p * 56 : (p + 1) * 56] = block[:, :56]
+    pressure_ref[...] = sum(basis[2 * k] * result[k] for k in range(3))
+    residual_ref[...] = basis[6] + sum(basis[2 * k + 1] * taken[k] for k in range(3))
 
     for step in range(ROUNDS):
         for copy in copies(step):
@@ -725,15 +738,16 @@
             pltpu.VMEM((ROUNDS, 4 * ES, LANES), jnp.float32),
             pltpu.VMEM((ROUNDS, 2, 4 * ES, LANES), jnp.float32),
             pltpu.VMEM((ROUNDS, 2, ES, LANES), jnp.float32),
-            pltpu.VMEM((len(stages), 8, 8, LANES), jnp.float32),
-            pltpu.VMEM((2, NP * ES, LANES), jnp.float32),
+            pltpu.VMEM((len(stages), PEERS, 8, LANES), jnp.float32),
+            pltpu.VMEM((7, NP * ES, LANES), jnp.float32),
+            pltpu.VMEM((7, A0, A1 * A2), jnp.float32),
             pltpu.SemaphoreType.DMA((ROUNDS, WAYS)),
             pltpu.SemaphoreType.DMA((ROUNDS, WAYS)),
-            pltpu.SemaphoreType.DMA((len(stages), 8)),
-            pltpu.SemaphoreType.DMA((len(stages), 8)),
+            pltpu.SemaphoreType.DMA((len(stages), PEERS)),
+            pltpu.SemaphoreType.DMA((len(stages), PEERS)),
         ],
         compiler_params=pltpu.CompilerParams(
-            collective_id=0, has_side_effects=True, vmem_limit_bytes=56 * 1024 * 1024
+            collective_id=0, has_side_effects=True, vmem_limit_bytes=55168 * 1024
         ),
     )(*operands)
 

time: 40.2 us -> 36.8 us (0.915)
  Pallas kernels: 36.6 us -> 34.1 us
  local copies, waits for them, and re-layouts: 2.72 us -> 1.87 us
    pallas_call x1, Pallas kernels: 36.6 us -> 34.1 us  [shards(): pl.pallas_call(functools.partial(kernel, count), out_shape=(block, block)...]
    unnamed x2 -> x4, local copies, waits for them, and re-layouts: 2.72 us -> 1.87 us
where the time goes in v3:
time: 36.8 us; the launch traced here: 36.6 us
  Pallas kernels  34.1 us (93%)
  local copies, waits for them, and re-layouts  1.87 us (5%)
  between operations  0.65 us (2%)
    pallas_call x1, Pallas kernels, shards(): pl.pallas_call(functools.partial(kernel, count), out_shape=(block, block)...  34.1 us
    unnamed x4, local copies, waits for them, and re-layouts  1.87 us

profile of v3, /device:TPU:0, one launch (start us, length us, event | category | flops | bytes accessed | tf_op | source)
XLA Modules:
  0.0 36.6 jit_solution(3698479668781366138)
XLA Ops:
  0.6 0.0 copy-start
  0.6 0.6 %copy-done = s32[16]{0:T(128)S(1)} copy-done((s32[16]{0:T(128)S(1)}, s32[16]{0:T(128)}, u32[]{:S(2)}) %copy-start) | copy-done | bytes 88
  1.3 34.1 %shard_map.86 = (f32[8,896]{1,0:T(8,128)S(1)}, f32[8,896]{1,0:T(8,128)S(1)}) custom-call(f32[3,3,16,512]{3,2,1,0:T(8,128)} %refs_0_.1, f32[2,3,16,512]{3,2,1,0:T(8,128)} %refs_1_.1, f32[3,16,512]{2,1,0:T(8,128)} %refs_2_.1, f32[16,512]{1,0:T(8,128)} %refs_3_.1, s32[1,16]{1,0:T(1,128)S(1)} %bitcast.1, bf16[6144,128]{1,0:T(8,128)(2,1)} %constant.4.clone.refs_5_, ...), custom_call_target="tpu_custom_call" | custom-call | tf_op jit(solution)/shard_map/pallas_call | solution.py:728
  35.4 0.6 %copy.11 = f32[8,896]{1,0:T(8,128)} copy(f32[8,896]{1,0:T(8,128)S(1)} %get-tuple-element.4) | data formatting | bytes 57344
  36.0 0.6 %copy.12 = f32[8,896]{1,0:T(8,128)} copy(f32[8,896]{1,0:T(8,128)S(1)} %get-tuple-element.5) | data formatting | bytes 57344
Async XLA Ops:
  0.6 0.7 %copy-start = (s32[16]{0:T(128)S(1)}, s32[16]{0:T(128)}, u32[]{:S(2)}) copy-start(s32[16]{0:T(128)} %param.11) | copy-start | bytes 196

commit v4 on v3

--- a/solution.py
+++ b/solution.py
@@ -281,6 +281,10 @@
         gathered,
         turned,
         basis,
+        inverses,
+        shares,
+        spaces,
+        dots,
         send_sem,
         recv_sem,
         gather_send_sem,
@@ -388,20 +392,15 @@
             )
         return stack(results)
 
-    def copies(step):
-        if step == 0:
+    def copies(step, first=False):
+        if first:
             plan = [(first_out.at[0], first_in.at[1], left), (first_out.at[1], first_in.at[0], right)]
-        elif step < ROUNDS - 1:
+        else:
             plan = [
                 (outbox.at[step, pl.ds(0, ES)], inbox_far.at[step, 1], far_left),
                 (outbox.at[step, pl.ds(3 * ES, ES)], inbox_far.at[step, 0], far_right),
                 (outbox.at[step], inbox.at[step, 1], left),
                 (outbox.at[step], inbox.at[step, 0], right),
-            ]
-        else:
-            plan = [
-                (outbox.at[step, pl.ds(0, ES)], inbox_far.at[step, 1], left),
-                (outbox.at[step, pl.ds(3 * ES, ES)], inbox_far.at[step, 0], right),
             ]
         return [
             pltpu.make_async_remote_copy(
@@ -434,13 +433,6 @@
                 parts[3] + jnp.where(low, 0.0, swap(after_it)),
             ]
         )
-
-    def surrounded(step, field):
-        receive(step)
-        beside = [inbox[step, 0], inbox[step, 1]]
-        ends = [inbox_far[step, 0], inbox_far[step, 1]]
-        own = axial_sum(field, beside[0][3 * ES :], beside[1][:ES])
-        return own, beside, ends
 
     def element_field(ref, *index):
         return stack([ref[index + (slice(None), pl.ds(j * LANES, LANES))] for j in range(4)])
@@ -544,20 +536,23 @@
     first_out[0] = stack([f[:ES] for f in around] + [flat, steep])
     first_out[1] = stack([f[3 * ES :] for f in around] + [flat, steep])
     pl.semaphore_wait(barrier, len(greeted))
-    for copy in copies(0):
+    for copy in copies(0, True):
         copy.start()
-    receive(0)
+    for copy in copies(0, True):
+        copy.wait_recv()
     lefts, rights = tiles(first_in[0]), tiles(first_in[1])
     summed = [axial_sum(around[f], lefts[f], rights[f]) for f in range(4)]
     accel = [lumps[d] * (summed[d] / summed[3]) for d in range(3)]
     divergence = gradient_t(accel[0], accel[1], accel[2])
-    source = around_sum(divergence)
-    send(1, source)
+    send(1, around_sum(divergence))
     loads[6].wait()
     flats = stack([lefts[4], flat, rights[4]])
     steeps = stack([lefts[5], steep, rights[5]])
     inverse = [1.0 / (steeps * float(eigen_axial[k]) + flats) for k in range(10)]
-    source, beside, ends = surrounded(1, source)
+    for k in range(10):
+        inverses[k] = inverse[k]
+    shares[...] = divergence
+    spaces[...] = jnp.zeros_like(spaces)
 
     def combine(weight, parts):
         acc = parts[0] * float(weight[0])
@@ -580,7 +575,7 @@
         for row, mode in zip(firsts, modes[1:]):
             grid[row], grid[row + 1] = mode[:, :LANES], mode[:, LANES:]
         order = [stack([grid[a - 7], grid[a], grid[a + 7]]) for a in range(-1, 9)]
-        spectra = [combine(solve[:, k], order) * inverse[k] for k in range(10)]
+        spectra = [combine(solve[:, k], order) * inverses[k] for k in range(10)]
         slabs = [[spectrum[b * ES : (b + 1) * ES] for spectrum in spectra] for b in range(3)]
         rows = [combine(solve[a + 1], slabs[1]) for a in range(NP)]
         rows[0] = rows[0] + combine(solve[8], slabs[0])
@@ -605,35 +600,32 @@
 
     def turn(which, field):
         for j, tile in enumerate(tiles(field)):
-            turned[which, pl.ds(2 * j * ES, ES)] = tile
-            turned[which, pl.ds((2 * j + 1) * ES, ES)] = swap(tile)
+            turned[pl.ds(2 * j * ES, ES)] = tile
+            turned[pl.ds((2 * j + 1) * ES, ES)] = swap(tile)
         for p in range(ES):
-            block = turned[which, pl.ds(p, NP, stride=ES), :]
+            block = turned[pl.ds(p, NP, stride=ES), :]
             basis[which, :, p * 56 : (p + 1) * 56] = block[:, :56]
 
-    spaces, images, dots = [], [], {}
-    current = source
-    for it in range(ITERS):
-        spaces.append(smooth(current, beside, ends))
-        local = apply(spaces[-1])
-        image = around_sum(local)
-        send(2 + it, image)
-        if it == 0:
-            head = inner(divergence, spaces[0])
-        for j in range(it + 1):
-            dots[j, it] = inner(local, spaces[j])
-        if it < ITERS - 1:
-            turn(2 * it, spaces[it])
-            if it == 0:
-                turn(6, current)
-            else:
-                turn(2 * it - 1, current)
-            current, beside, ends = surrounded(2 + it, image)
-            images.append(current)
-
+    def iteration(it, carry):
+        step = it + 1
+        receive(step)
+        beside = [inbox[step, 0], inbox[step, 1]]
+        ends = [inbox_far[step, 0], inbox_far[step, 1]]
+        current = axial_sum(outbox[step], beside[0][3 * ES :], beside[1][:ES])
+        space = smooth(current, beside, ends)
+        local = apply(space)
+        spaces[it] = space
+        send(step + 1, around_sum(local))
+        dots[it] = jnp.concatenate([inner(local, spaces[j]) for j in range(ITERS)], axis=0)
+        turn(2 * it, current)
+        turn(2 * it + 1, space)
+        return carry
+
+    lax.fori_loop(0, ITERS, iteration, 0)
+    head = inner(shares[...], spaces[0])
     value = jnp.concatenate(
         [head]
-        + [dots[i, j] for i in range(3) for j in range(i, 3)]
+        + [dots[j, i : i + 1] for i in range(3) for j in range(i, 3)]
         + [jnp.zeros((1, LANES), jnp.float32)],
         axis=0,
     )
@@ -653,11 +645,11 @@
             copy.start()
             started.append(copy)
         if stage == 0:
-            turn(4, spaces[2])
-            turn(3, images[1])
-            receive(ROUNDS - 1)
-            ends = [inbox_far[ROUNDS - 1, 0], inbox_far[ROUNDS - 1, 1]]
-            turn(5, axial_sum(image, ends[0], ends[1]))
+            last = ROUNDS - 1
+            receive(last)
+            turn(
+                6, axial_sum(outbox[last], inbox[last, 0, 3 * ES :], inbox[last, 1, :ES])
+            )
         for copy in started[1 - size :]:
             copy.wait_recv()
         value = gathered[stage, 0]
@@ -707,11 +699,11 @@
             result[k] = step if result[k] is None else result[k] + step
             taken[k] = -step if taken[k] is None else taken[k] - step
         previous = rho
-    pressure_ref[...] = sum(basis[2 * k] * result[k] for k in range(3))
-    residual_ref[...] = basis[6] + sum(basis[2 * k + 1] * taken[k] for k in range(3))
+    pressure_ref[...] = sum(basis[2 * k + 1] * result[k] for k in range(3))
+    residual_ref[...] = basis[0] + sum(basis[2 * k + 2] * taken[k] for k in range(3))
 
     for step in range(ROUNDS):
-        for copy in copies(step):
+        for copy in copies(step, step == 0):
             copy.wait_send()
     for copy in started:
         copy.wait_send()
@@ -739,8 +731,12 @@
             pltpu.VMEM((ROUNDS, 2, 4 * ES, LANES), jnp.float32),
             pltpu.VMEM((ROUNDS, 2, ES, LANES), jnp.float32),
             pltpu.VMEM((len(stages), PEERS, 8, LANES), jnp.float32),
-            pltpu.VMEM((7, NP * ES, LANES), jnp.float32),
+            pltpu.VMEM((NP * ES, LANES), jnp.float32),
             pltpu.VMEM((7, A0, A1 * A2), jnp.float32),
+            pltpu.VMEM((10, 3 * ES, LANES), jnp.float32),
+            pltpu.VMEM((4 * ES, LANES), jnp.float32),
+            pltpu.VMEM((ITERS, 4 * ES, LANES), jnp.float32),
+            pltpu.VMEM((ITERS, ITERS, LANES), jnp.float32),
             pltpu.SemaphoreType.DMA((ROUNDS, WAYS)),
             pltpu.SemaphoreType.DMA((ROUNDS, WAYS)),
             pltpu.SemaphoreType.DMA((len(stages), PEERS)),

time: 36.8 us -> 37.2 us (1.011)
  Pallas kernels: 34.1 us -> 34.5 us
    pallas_call x1, Pallas kernels: 34.1 us -> 34.5 us  [shards(): pl.pallas_call(functools.partial(kernel, count), out_shape=(block, block)...]
where the time goes in v4:
time: 37.2 us; the launch traced here: 37 us
  Pallas kernels  34.5 us (93%)
  local copies, waits for them, and re-layouts  1.87 us (5%)
  between operations  0.65 us (2%)
    pallas_call x1, Pallas kernels, shards(): pl.pallas_call(functools.partial(kernel, count), out_shape=(block, block)...  34.5 us
    unnamed x4, local copies, waits for them, and re-layouts  1.87 us

profile of v4, /device:TPU:0, one launch (start us, length us, event | category | flops | bytes accessed | tf_op | source)
XLA Modules:
  0.0 37.0 jit_solution(9906200664131543664)
XLA Ops:
  0.6 0.0 copy-start
  0.6 0.6 %copy-done = s32[16]{0:T(128)S(1)} copy-done((s32[16]{0:T(128)S(1)}, s32[16]{0:T(128)}, u32[]{:S(2)}) %copy-start) | copy-done | bytes 88
  1.3 34.5 %shard_map.86 = (f32[8,896]{1,0:T(8,128)S(1)}, f32[8,896]{1,0:T(8,128)S(1)}) custom-call(f32[3,3,16,512]{3,2,1,0:T(8,128)} %refs_0_.1, f32[2,3,16,512]{3,2,1,0:T(8,128)} %refs_1_.1, f32[3,16,512]{2,1,0:T(8,128)} %refs_2_.1, f32[16,512]{1,0:T(8,128)} %refs_3_.1, s32[1,16]{1,0:T(1,128)S(1)} %bitcast.1, bf16[6144,128]{1,0:T(8,128)(2,1)} %constant.4.clone.refs_5_, ...), custom_call_target="tpu_custom_call" | custom-call | tf_op jit(solution)/shard_map/pallas_call | solution.py:720
  35.8 0.6 %copy.11 = f32[8,896]{1,0:T(8,128)} copy(f32[8,896]{1,0:T(8,128)S(1)} %get-tuple-element.4) | data formatting | bytes 57344
  36.4 0.6 %copy.12 = f32[8,896]{1,0:T(8,128)} copy(f32[8,896]{1,0:T(8,128)S(1)} %get-tuple-element.5) | data formatting | bytes 57344
Async XLA Ops:
  0.6 0.7 %copy-start = (s32[16]{0:T(128)S(1)}, s32[16]{0:T(128)}, u32[]{:S(2)}) copy-start(s32[16]{0:T(128)} %param.11) | copy-start | bytes 196

commit v5 on v3

--- a/solution.py
+++ b/solution.py
@@ -17,7 +17,7 @@
 A2 = 8
 ROUNDS = 5
 WAYS = 4
-PEERS = 32
+PEERS = 8
 LANES = 128
 MESH = pl.DeviceIdType.MESH
 

time: 36.8 us -> 38.6 us (1.049)
  Pallas kernels: 34.1 us -> 35.9 us
    pallas_call x1, Pallas kernels: 34.1 us -> 35.9 us  [shards(): pl.pallas_call(functools.partial(kernel, count), out_shape=(block, block)...]
where the time goes in v5:
time: 38.6 us; the launch traced here: 38.4 us
  Pallas kernels  35.9 us (93%)
  local copies, waits for them, and re-layouts  1.87 us (5%)
  between operations  0.65 us (2%)
    pallas_call x1, Pallas kernels, shards(): pl.pallas_call(functools.partial(kernel, count), out_shape=(block, block)...  35.9 us
    unnamed x4, local copies, waits for them, and re-layouts  1.87 us

profile of v5, /device:TPU:0, one launch (start us, length us, event | category | flops | bytes accessed | tf_op | source)
XLA Modules:
  0.0 38.4 jit_solution(10694348653157501842)
XLA Ops:
  0.6 0.0 copy-start
  0.6 0.6 %copy-done = s32[16]{0:T(128)S(1)} copy-done((s32[16]{0:T(128)S(1)}, s32[16]{0:T(128)}, u32[]{:S(2)}) %copy-start) | copy-done | bytes 88
  1.3 35.9 %shard_map.86 = (f32[8,896]{1,0:T(8,128)S(1)}, f32[8,896]{1,0:T(8,128)S(1)}) custom-call(f32[3,3,16,512]{3,2,1,0:T(8,128)} %refs_0_.1, f32[2,3,16,512]{3,2,1,0:T(8,128)} %refs_1_.1, f32[3,16,512]{2,1,0:T(8,128)} %refs_2_.1, f32[16,512]{1,0:T(8,128)} %refs_3_.1, s32[1,16]{1,0:T(1,128)S(1)} %bitcast.1, bf16[6144,128]{1,0:T(8,128)(2,1)} %constant.4.clone.refs_5_, ...), custom_call_target="tpu_custom_call" | custom-call | tf_op jit(solution)/shard_map/pallas_call | solution.py:728
  37.2 0.6 %copy.11 = f32[8,896]{1,0:T(8,128)} copy(f32[8,896]{1,0:T(8,128)S(1)} %get-tuple-element.4) | data formatting | bytes 57344
  37.8 0.6 %copy.12 = f32[8,896]{1,0:T(8,128)} copy(f32[8,896]{1,0:T(8,128)S(1)} %get-tuple-element.5) | data formatting | bytes 57344
Async XLA Ops:
  0.6 0.7 %copy-start = (s32[16]{0:T(128)S(1)}, s32[16]{0:T(128)}, u32[]{:S(2)}) copy-start(s32[16]{0:T(128)} %param.11) | copy-start | bytes 196

commit v6 on v3

--- a/solution.py
+++ b/solution.py
@@ -16,7 +16,7 @@
 A1 = 112
 A2 = 8
 ROUNDS = 5
-WAYS = 4
+WAYS = 6
 PEERS = 32
 LANES = 128
 MESH = pl.DeviceIdType.MESH
@@ -223,7 +223,7 @@
     weights = np.concatenate(
         [split_rows(m) for m in (pair, pair.T, fine, fine_slope, fine.T, ahead, back.T)]
     )
-    along = np.concatenate([halves(d), halves(d.T), halves(itp), halves(slope), halves(itp.T)])
+    along = np.concatenate([halves(d), halves(d.T), halves(itp), halves(slope), halves(itp.T), halves(d[[0, -1]].T)])
     fine_mass = np.repeat(fine_mass, ES, axis=0)
     tables = np.concatenate(
         [along, nodes]
@@ -245,8 +245,8 @@
 FINE_T = (3328, 384, 128)
 AHEAD = (4096, 256, 256)
 BACK = (5120, 256, 256)
-TABLE_NODES, TABLE_FINE, TABLE_EIGEN = 208, 272, 560
-COEF_D, COEF_DT, COEF_I, COEF_S, COEF_IT = 0, 32, 64, 112, 160
+TABLE_NODES, TABLE_FINE, TABLE_EIGEN = 216, 280, 568
+COEF_D, COEF_DT, COEF_I, COEF_S, COEF_IT, COEF_FACE = 0, 32, 64, 112, 160, 208
 
 
 OPERANDS = 7
@@ -273,8 +273,13 @@
     held, refs = refs[2 : 2 + OPERANDS], refs[2 + OPERANDS :]
     (
         load_sem,
-        first_out,
-        first_in,
+        early_out,
+        early_in,
+        early_third,
+        main_out,
+        main_in,
+        main_second,
+        main_third,
         outbox,
         inbox,
         inbox_far,
@@ -296,7 +301,7 @@
                 operands[which].at[rows], held[which].at[rows], load_sem.at[i]
             )
         )
-    for i in (3, 2, 0, 7, 5, 1, 4, 6):
+    for i in (3, 7, 4, 2, 0, 5, 1, 6):
         loads[i].start()
     velocity, past, metric, jacobian, slots, weights, tables = held
 
@@ -306,6 +311,8 @@
     right = lax.rem(me + 1, count)
     far_left = lax.rem(me + count - 2, count)
     far_right = lax.rem(me + 2, count)
+    third_left = lax.rem(me + count - 3, count)
+    third_right = lax.rem(me + 3, count)
     stages = stages_of(count)
 
     def peer(stage, offset):
@@ -315,7 +322,7 @@
         return me + (other - digit) * stride
 
     barrier = pltpu.get_barrier_semaphore()
-    greeted = [left, right, far_left, far_right] + [
+    greeted = [left, right, far_left, far_right, third_left, third_right] + [
         peer(stage, offset)
         for stage in range(len(stages))
         for offset in range(1, stages[stage][1])
@@ -390,7 +397,25 @@
 
     def copies(step):
         if step == 0:
-            plan = [(first_out.at[0], first_in.at[1], left), (first_out.at[1], first_in.at[0], right)]
+            face = early_out.at[pl.ds(0, ES)]
+            plan = [
+                (face, early_third.at[1], third_left),
+                (face, early_third.at[0], third_right),
+                (early_out, early_in.at[3], far_left),
+                (early_out, early_in.at[0], far_right),
+                (early_out, early_in.at[2], left),
+                (early_out, early_in.at[1], right),
+            ]
+        elif step == 1:
+            face = main_out.at[pl.ds(ES, ES)]
+            plan = [
+                (face, main_third.at[1], third_left),
+                (face, main_third.at[0], third_right),
+                (main_out.at[pl.ds(0, 4 * ES)], main_second.at[1], far_left),
+                (main_out.at[pl.ds(ES, 4 * ES)], main_second.at[0], far_right),
+                (main_out, main_in.at[1], left),
+                (main_out, main_in.at[0], right),
+            ]
         elif step < ROUNDS - 1:
             plan = [
                 (outbox.at[step, pl.ds(0, ES)], inbox_far.at[step, 1], far_left),
@@ -445,6 +470,12 @@
     def element_field(ref, *index):
         return stack([ref[index + (slice(None), pl.ds(j * LANES, LANES))] for j in range(4)])
 
+    def faces(field):
+        return jnp.where(low, field[:ES], field[3 * ES :])
+
+    def across(before_it, after_it):
+        return jnp.where(low, swap(before_it), swap(after_it))
+
     loads[7].wait()
     loads[3].wait()
     weight3 = tables[TABLE_NODES:TABLE_FINE]
@@ -462,6 +493,46 @@
     newest = [element_field(velocity, 0, i) for i in range(3)]
     coarse += [along(newest[d] * metrics[d], COEF_I, 6) for d in range(3)]
     coarse += [along(newest[i], COEF_S, 6) for i in range(3)]
+    loads[4].wait()
+    position = lax.broadcasted_iota(jnp.int32, (ES, ES), 0)
+    chosen = jnp.where(slots[...] == position, 1.0, 0.0)
+    chosen = jnp.concatenate([chosen, chosen, chosen], axis=1).astype(jnp.bfloat16)
+
+    def into_order(fields):
+        wide = jnp.concatenate([tile for field in fields for tile in tiles(field)], axis=1)
+        first = wide.astype(jnp.bfloat16)
+        rest = wide - first.astype(jnp.float32)
+        second = rest.astype(jnp.bfloat16)
+        third = (rest - second.astype(jnp.float32)).astype(jnp.bfloat16)
+        placed = jnp.dot(
+            chosen, stack([first, second, third]), preferred_element_type=jnp.float32
+        )
+        return [
+            stack([placed[:, (4 * f + j) * LANES : (4 * f + j + 1) * LANES] for j in range(4)])
+            for f in range(len(fields))
+        ]
+
+    placed_mass, *placed_metrics = into_order([mass] + metrics)
+    placed_lumps = [placed_mass * m for m in placed_metrics]
+    placed_squares = [placed_lumps[d] * placed_metrics[d] for d in range(3)]
+
+    def total(field):
+        parts = tiles(field)
+        return jnp.sum(parts[0] + parts[1] + parts[2] + parts[3], axis=1, keepdims=True) / 8.0
+
+    flat = (
+        total(placed_squares[1]) * eigen[0:1]
+        + total(placed_squares[2]) * eigen[1:2]
+        + mass_shift * total(placed_mass)
+    )
+    steep = jnp.broadcast_to(total(placed_squares[0]), (ES, LANES))
+    mass_around = around_sum(placed_mass)
+    early = [faces(mass_around)] + [faces(lump) for lump in placed_lumps] + [flat, steep]
+    early_out[...] = stack(early)
+    pl.semaphore_wait(barrier, len(greeted))
+    for copy in copies(0):
+        copy.start()
+
     loads[5].wait()
     fine = mm(stack(coarse), FINE)
     fine = [fine[i * 96 : (i + 1) * 96] for i in range(7)]
@@ -494,7 +565,6 @@
     paired_t = mm(slopes, PAIR_T)
     forcing = []
     loads[1].wait()
-    loads[4].wait()
     for i in range(3):
         convect = along(advected[i * 96 : (i + 1) * 96], COEF_IT, 4)
         stiff = paired_t[i * 64 : (i + 1) * 64] + along(
@@ -511,53 +581,67 @@
         helmholtz = viscosity * stiff + 11.0 / (6.0 * time_step) * mass * guessed[i]
         forcing.append(mass * history / time_step - extrap - helmholtz)
 
-    fields = forcing + [mass] + metrics
-    wide = jnp.concatenate([tile for field in fields for tile in tiles(field)], axis=1)
-    first = wide.astype(jnp.bfloat16)
-    rest = wide - first.astype(jnp.float32)
-    second = rest.astype(jnp.bfloat16)
-    third = (rest - second.astype(jnp.float32)).astype(jnp.bfloat16)
-    position = lax.broadcasted_iota(jnp.int32, (ES, ES), 0)
-    chosen = jnp.where(slots[...] == position, 1.0, 0.0)
-    chosen = jnp.concatenate([chosen, chosen, chosen], axis=1).astype(jnp.bfloat16)
-    placed = jnp.dot(chosen, stack([first, second, third]), preferred_element_type=jnp.float32)
-    fields = [
-        stack([placed[:, (4 * f + j) * LANES : (4 * f + j + 1) * LANES] for j in range(4)])
-        for f in range(7)
-    ]
-    forcing, mass, metrics = fields[:3], fields[3], fields[4:]
-    lumps = [mass * m for m in metrics]
-    squares = [lumps[d] * metrics[d] for d in range(3)]
-
-    def total(field):
-        parts = tiles(field)
-        return jnp.sum(parts[0] + parts[1] + parts[2] + parts[3], axis=1, keepdims=True) / 8.0
-
-    flat = (
-        total(squares[1]) * eigen[0:1]
-        + total(squares[2]) * eigen[1:2]
-        + mass_shift * total(mass)
-    )
-    steep = jnp.broadcast_to(total(squares[0]), (ES, LANES))
-
-    around = [around_sum(f) for f in forcing + [mass]]
-    first_out[0] = stack([f[:ES] for f in around] + [flat, steep])
-    first_out[1] = stack([f[3 * ES :] for f in around] + [flat, steep])
-    pl.semaphore_wait(barrier, len(greeted))
+    (f0, f1, f2) = into_order(forcing)
+    around = [around_sum(f) for f in (f0, f1, f2)]
     for copy in copies(0):
+        copy.wait_recv()
+    shown = [tiles(early_in[i]) for i in range(4)]
+    shown = [shown[0], shown[1], early, shown[2], shown[3]]
+    mass_faces = [early_third[0]] + [one[0] for one in shown] + [early_third[1]]
+    total_mass = axial_sum(mass_around, mass_faces[2], mass_faces[4])
+    accel = [placed_lumps[d] * (around[d] / total_mass) for d in range(3)]
+    partial = gradient_t(accel[0], accel[1], accel[2])
+    parts = tiles(partial)
+    own_faces = [faces(f) for f in around]
+    main_out[...] = stack([parts[0]] + own_faces + [parts[3], parts[1], parts[2]])
+    for copy in copies(1):
         copy.start()
-    receive(0)
-    lefts, rights = tiles(first_in[0]), tiles(first_in[1])
-    summed = [axial_sum(around[f], lefts[f], rights[f]) for f in range(4)]
-    accel = [lumps[d] * (summed[d] / summed[3]) for d in range(3)]
-    divergence = gradient_t(accel[0], accel[1], accel[2])
-    source = around_sum(divergence)
-    send(1, source)
     loads[6].wait()
+    lump_faces = []
+    for b in range(5):
+        ratio = mass_faces[b + 1] + across(mass_faces[b], mass_faces[b + 2])
+        lump_faces.append([shown[b][1 + d] / ratio for d in range(3)])
+    lefts, rights = shown[1], shown[3]
     flats = stack([lefts[4], flat, rights[4]])
     steeps = stack([lefts[5], steep, rights[5]])
     inverse = [1.0 / (steeps * float(eigen_axial[k]) + flats) for k in range(10)]
-    source, beside, ends = surrounded(1, source)
+    for copy in copies(1):
+        copy.wait_recv()
+    lower, upper = tiles(main_in[0]), tiles(main_in[1])
+    beyond = [tiles(main_second[0]), tiles(main_second[1])]
+    none = jnp.zeros((ES, LANES), jnp.float32)
+    force_faces = [
+        [main_third[0], none, none],
+        beyond[0][:3],
+        lower[1:4],
+        own_faces,
+        upper[1:4],
+        beyond[1][1:],
+        [main_third[1], none, none],
+    ]
+    added = [
+        [lump_faces[b][d] * across(force_faces[b][d], force_faces[b + 2][d]) for d in range(3)]
+        for b in range(5)
+    ]
+    sides = tiles(
+        mm(
+            jnp.concatenate([stack([a[1] for a in added]), stack([a[2] for a in added])], axis=1),
+            PAIR_T,
+        )
+    )
+    whole = []
+    for b in range(5):
+        extra = tiles(along(added[b][0], COEF_FACE, 4))
+        extra[0] = extra[0] + jnp.where(low, sides[b], 0.0)
+        extra[3] = extra[3] + jnp.where(low, 0.0, sides[b])
+        whole.append(extra)
+    divergence = partial + stack(whole[2])
+    beside = [
+        around_sum(stack([near[0], near[5], near[6], near[4]]) + stack(extra))
+        for near, extra in ((lower, whole[1]), (upper, whole[3]))
+    ]
+    ends = [around_sum(beyond[0][3] + whole[0][3]), around_sum(beyond[1][0] + whole[4][0])]
+    source = axial_sum(around_sum(divergence), beside[0][3 * ES :], beside[1][:ES])
 
     def combine(weight, parts):
         acc = parts[0] * float(weight[0])
@@ -597,8 +681,10 @@
 
     def apply(field):
         axial, around, radial = gradient(field)
-        local = gradient_t(squares[0] * axial, squares[1] * around, squares[2] * radial)
-        return local + mass_shift * mass * field
+        local = gradient_t(
+            placed_squares[0] * axial, placed_squares[1] * around, placed_squares[2] * radial
+        )
+        return local + mass_shift * placed_mass * field
 
     def inner(one, two):
         return jnp.sum(one * two, axis=0, keepdims=True)
@@ -733,8 +819,13 @@
         scratch_shapes=[pltpu.VMEM(x.shape, x.dtype) for x in operands]
         + [
             pltpu.SemaphoreType.DMA((len(operands) + 1,)),
-            pltpu.VMEM((2, 6 * ES, LANES), jnp.float32),
-            pltpu.VMEM((2, 6 * ES, LANES), jnp.float32),
+            pltpu.VMEM((6 * ES, LANES), jnp.float32),
+            pltpu.VMEM((4, 6 * ES, LANES), jnp.float32),
+            pltpu.VMEM((2, ES, LANES), jnp.float32),
+            pltpu.VMEM((7 * ES, LANES), jnp.float32),
+            pltpu.VMEM((2, 7 * ES, LANES), jnp.float32),
+            pltpu.VMEM((2, 4 * ES, LANES), jnp.float32),
+            pltpu.VMEM((2, ES, LANES), jnp.float32),
             pltpu.VMEM((ROUNDS, 4 * ES, LANES), jnp.float32),
             pltpu.VMEM((ROUNDS, 2, 4 * ES, LANES), jnp.float32),
             pltpu.VMEM((ROUNDS, 2, ES, LANES), jnp.float32),

time: 36.8 us -> 37.8 us (1.027)
  Pallas kernels: 34.1 us -> 35.2 us
    pallas_call x1, Pallas kernels: 34.1 us -> 35.2 us  [shards(): pl.pallas_call(functools.partial(kernel, count), out_shape=(block, block)...]
where the time goes in v6:
time: 37.8 us; the launch traced here: 37.7 us
  Pallas kernels  35.2 us (93%)
  local copies, waits for them, and re-layouts  1.87 us (5%)
  between operations  0.65 us (2%)
    pallas_call x1, Pallas kernels, shards(): pl.pallas_call(functools.partial(kernel, count), out_shape=(block, block)...  35.2 us
    unnamed x4, local copies, waits for them, and re-layouts  1.87 us

profile of v6, /device:TPU:0, one launch (start us, length us, event | category | flops | bytes accessed | tf_op | source)
XLA Modules:
  0.0 37.7 jit_solution(16780536660849911848)
XLA Ops:
  0.6 0.0 copy-start
  0.6 0.6 %copy-done = s32[16]{0:T(128)S(1)} copy-done((s32[16]{0:T(128)S(1)}, s32[16]{0:T(128)}, u32[]{:S(2)}) %copy-start) | copy-done | bytes 88
  1.3 35.2 %shard_map.86 = (f32[8,896]{1,0:T(8,128)S(1)}, f32[8,896]{1,0:T(8,128)S(1)}) custom-call(f32[3,3,16,512]{3,2,1,0:T(8,128)} %refs_0_.1, f32[2,3,16,512]{3,2,1,0:T(8,128)} %refs_1_.1, f32[3,16,512]{2,1,0:T(8,128)} %refs_2_.1, f32[16,512]{1,0:T(8,128)} %refs_3_.1, s32[1,16]{1,0:T(1,128)S(1)} %bitcast.1, bf16[6144,128]{1,0:T(8,128)(2,1)} %constant.4.clone.refs_5_, ...), custom_call_target="tpu_custom_call" | custom-call | tf_op jit(solution)/shard_map/pallas_call | solution.py:814
  36.5 0.6 %copy.11 = f32[8,896]{1,0:T(8,128)} copy(f32[8,896]{1,0:T(8,128)S(1)} %get-tuple-element.4) | data formatting | bytes 57344
  37.1 0.6 %copy.12 = f32[8,896]{1,0:T(8,128)} copy(f32[8,896]{1,0:T(8,128)S(1)} %get-tuple-element.5) | data formatting | bytes 57344
Async XLA Ops:
  0.6 0.7 %copy-start = (s32[16]{0:T(128)S(1)}, s32[16]{0:T(128)}, u32[]{:S(2)}) copy-start(s32[16]{0:T(128)} %param.11) | copy-start | bytes 196

commit v7 on v3

--- a/solution.py
+++ b/solution.py
@@ -637,14 +637,19 @@
         + [jnp.zeros((1, LANES), jnp.float32)],
         axis=0,
     )
+    sums = jnp.sum(value, axis=1, keepdims=True)
+    row8 = lax.broadcasted_iota(jnp.int32, (8, LANES), 0)
+    lane8 = lax.broadcasted_iota(jnp.int32, (8, LANES), 1)
+    value = jnp.sum(jnp.where(row8 == lane8, sums, 0.0), axis=0, keepdims=True)
     started = []
     for stage, (stride, size) in enumerate(stages):
         digit = lax.rem(me // stride, size)
-        gathered[stage, digit] = value
+        slot = gathered.at[stage, pl.ds(digit, 1)]
+        slot[...] = value
         for offset in range(1, size):
             copy = pltpu.make_async_remote_copy(
-                src_ref=gathered.at[stage, digit],
-                dst_ref=gathered.at[stage, digit],
+                src_ref=slot,
+                dst_ref=slot,
                 send_sem=gather_send_sem.at[stage, offset],
                 recv_sem=gather_recv_sem.at[stage, offset],
                 device_id=(peer(stage, offset),),
@@ -660,11 +665,8 @@
             turn(5, axial_sum(image, ends[0], ends[1]))
         for copy in started[1 - size :]:
             copy.wait_recv()
-        value = gathered[stage, 0]
-        for slot in range(1, size):
-            value = value + gathered[stage, slot]
-    sums = jnp.sum(value, axis=1, keepdims=True)
-    sums = [sums[i : i + 1] for i in range(7)]
+        value = jnp.sum(gathered[stage, :size], axis=0, keepdims=True)
+    sums = [value[:, i : i + 1] for i in range(7)]
     gram = {}
     for at, (i, j) in enumerate([(i, j) for i in range(3) for j in range(i, 3)]):
         gram[i, j] = gram[j, i] = sums[1 + at]
@@ -738,7 +740,7 @@
             pltpu.VMEM((ROUNDS, 4 * ES, LANES), jnp.float32),
             pltpu.VMEM((ROUNDS, 2, 4 * ES, LANES), jnp.float32),
             pltpu.VMEM((ROUNDS, 2, ES, LANES), jnp.float32),
-            pltpu.VMEM((len(stages), PEERS, 8, LANES), jnp.float32),
+            pltpu.VMEM((len(stages), PEERS, LANES), jnp.float32),
             pltpu.VMEM((7, NP * ES, LANES), jnp.float32),
             pltpu.VMEM((7, A0, A1 * A2), jnp.float32),
             pltpu.SemaphoreType.DMA((ROUNDS, WAYS)),

time: 36.8 us -> 36.8 us (level)
  no operation moved by 1% of the time
where the time goes in v7:
time: 36.8 us; the launch traced here: 36.6 us
  Pallas kernels  34.1 us (93%)
  local copies, waits for them, and re-layouts  1.87 us (5%)
  between operations  0.65 us (2%)
    pallas_call x1, Pallas kernels, shards(): pl.pallas_call(functools.partial(kernel, count), out_shape=(block, block)...  34.1 us
    unnamed x4, local copies, waits for them, and re-layouts  1.87 us

profile of v7, /device:TPU:0, one launch (start us, length us, event | category | flops | bytes accessed | tf_op | source)
XLA Modules:
  0.0 36.6 jit_solution(9844068843090825869)
XLA Ops:
  0.6 0.0 copy-start
  0.6 0.6 %copy-done = s32[16]{0:T(128)S(1)} copy-done((s32[16]{0:T(128)S(1)}, s32[16]{0:T(128)}, u32[]{:S(2)}) %copy-start) | copy-done | bytes 88
  1.3 34.1 %shard_map.86 = (f32[8,896]{1,0:T(8,128)S(1)}, f32[8,896]{1,0:T(8,128)S(1)}) custom-call(f32[3,3,16,512]{3,2,1,0:T(8,128)} %refs_0_.1, f32[2,3,16,512]{3,2,1,0:T(8,128)} %refs_1_.1, f32[3,16,512]{2,1,0:T(8,128)} %refs_2_.1, f32[16,512]{1,0:T(8,128)} %refs_3_.1, s32[1,16]{1,0:T(1,128)S(1)} %bitcast.1, bf16[6144,128]{1,0:T(8,128)(2,1)} %constant.4.clone.refs_5_, ...), custom_call_target="tpu_custom_call" | custom-call | tf_op jit(solution)/shard_map/pallas_call | solution.py:730
  35.4 0.6 %copy.11 = f32[8,896]{1,0:T(8,128)} copy(f32[8,896]{1,0:T(8,128)S(1)} %get-tuple-element.4) | data formatting | bytes 57344
  36.0 0.6 %copy.12 = f32[8,896]{1,0:T(8,128)} copy(f32[8,896]{1,0:T(8,128)S(1)} %get-tuple-element.5) | data formatting | bytes 57344
Async XLA Ops:
  0.6 0.7 %copy-start = (s32[16]{0:T(128)S(1)}, s32[16]{0:T(128)}, u32[]{:S(2)}) copy-start(s32[16]{0:T(128)} %param.11) | copy-start | bytes 196

commit v8 on v6

--- a/solution.py
+++ b/solution.py
@@ -276,6 +276,7 @@
         early_out,
         early_in,
         early_third,
+        mass_in,
         main_out,
         main_in,
         main_second,
@@ -406,6 +407,9 @@
                 (early_out, early_in.at[2], left),
                 (early_out, early_in.at[1], right),
             ]
+        elif step == ROUNDS:
+            face = early_out.at[pl.ds(0, ES)]
+            plan = [(face, mass_in.at[1], left), (face, mass_in.at[0], right)]
         elif step == 1:
             face = main_out.at[pl.ds(ES, ES)]
             plan = [
@@ -485,14 +489,8 @@
     eigen = tables[TABLE_EIGEN:]
     jac = element_field(jacobian)
     mass = jac * weight3
-    coarse = [along(jac, COEF_I, 6)]
     loads[2].wait()
     metrics = [element_field(metric, d) for d in range(3)]
-    squares = [mass * m * m for m in metrics]
-    loads[0].wait()
-    newest = [element_field(velocity, 0, i) for i in range(3)]
-    coarse += [along(newest[d] * metrics[d], COEF_I, 6) for d in range(3)]
-    coarse += [along(newest[i], COEF_S, 6) for i in range(3)]
     loads[4].wait()
     position = lax.broadcasted_iota(jnp.int32, (ES, ES), 0)
     chosen = jnp.where(slots[...] == position, 1.0, 0.0)
@@ -530,9 +528,15 @@
     early = [faces(mass_around)] + [faces(lump) for lump in placed_lumps] + [flat, steep]
     early_out[...] = stack(early)
     pl.semaphore_wait(barrier, len(greeted))
-    for copy in copies(0):
+    for copy in copies(ROUNDS) + copies(0):
         copy.start()
 
+    coarse = [along(jac, COEF_I, 6)]
+    squares = [mass * m * m for m in metrics]
+    loads[0].wait()
+    newest = [element_field(velocity, 0, i) for i in range(3)]
+    coarse += [along(newest[d] * metrics[d], COEF_I, 6) for d in range(3)]
+    coarse += [along(newest[i], COEF_S, 6) for i in range(3)]
     loads[5].wait()
     fine = mm(stack(coarse), FINE)
     fine = [fine[i * 96 : (i + 1) * 96] for i in range(7)]
@@ -583,12 +587,9 @@
 
     (f0, f1, f2) = into_order(forcing)
     around = [around_sum(f) for f in (f0, f1, f2)]
-    for copy in copies(0):
+    for copy in copies(ROUNDS):
         copy.wait_recv()
-    shown = [tiles(early_in[i]) for i in range(4)]
-    shown = [shown[0], shown[1], early, shown[2], shown[3]]
-    mass_faces = [early_third[0]] + [one[0] for one in shown] + [early_third[1]]
-    total_mass = axial_sum(mass_around, mass_faces[2], mass_faces[4])
+    total_mass = axial_sum(mass_around, mass_in[0], mass_in[1])
     accel = [placed_lumps[d] * (around[d] / total_mass) for d in range(3)]
     partial = gradient_t(accel[0], accel[1], accel[2])
     parts = tiles(partial)
@@ -596,6 +597,11 @@
     main_out[...] = stack([parts[0]] + own_faces + [parts[3], parts[1], parts[2]])
     for copy in copies(1):
         copy.start()
+    for copy in copies(0):
+        copy.wait_recv()
+    shown = [tiles(early_in[i]) for i in range(4)]
+    shown = [shown[0], shown[1], early, shown[2], shown[3]]
+    mass_faces = [early_third[0]] + [one[0] for one in shown] + [early_third[1]]
     loads[6].wait()
     lump_faces = []
     for b in range(5):
@@ -723,14 +729,19 @@
         + [jnp.zeros((1, LANES), jnp.float32)],
         axis=0,
     )
+    sums = jnp.sum(value, axis=1, keepdims=True)
+    row8 = lax.broadcasted_iota(jnp.int32, (8, LANES), 0)
+    lane8 = lax.broadcasted_iota(jnp.int32, (8, LANES), 1)
+    value = jnp.sum(jnp.where(row8 == lane8, sums, 0.0), axis=0, keepdims=True)
     started = []
     for stage, (stride, size) in enumerate(stages):
         digit = lax.rem(me // stride, size)
-        gathered[stage, digit] = value
+        slot = gathered.at[stage, pl.ds(digit, 1)]
+        slot[...] = value
         for offset in range(1, size):
             copy = pltpu.make_async_remote_copy(
-                src_ref=gathered.at[stage, digit],
-                dst_ref=gathered.at[stage, digit],
+                src_ref=slot,
+                dst_ref=slot,
                 send_sem=gather_send_sem.at[stage, offset],
                 recv_sem=gather_recv_sem.at[stage, offset],
                 device_id=(peer(stage, offset),),
@@ -746,11 +757,8 @@
             turn(5, axial_sum(image, ends[0], ends[1]))
         for copy in started[1 - size :]:
             copy.wait_recv()
-        value = gathered[stage, 0]
-        for slot in range(1, size):
-            value = value + gathered[stage, slot]
-    sums = jnp.sum(value, axis=1, keepdims=True)
-    sums = [sums[i : i + 1] for i in range(7)]
+        value = jnp.sum(gathered[stage, :size], axis=0, keepdims=True)
+    sums = [value[:, i : i + 1] for i in range(7)]
     gram = {}
     for at, (i, j) in enumerate([(i, j) for i in range(3) for j in range(i, 3)]):
         gram[i, j] = gram[j, i] = sums[1 + at]
@@ -796,7 +804,7 @@
     pressure_ref[...] = sum(basis[2 * k] * result[k] for k in range(3))
     residual_ref[...] = basis[6] + sum(basis[2 * k + 1] * taken[k] for k in range(3))
 
-    for step in range(ROUNDS):
+    for step in range(ROUNDS + 1):
         for copy in copies(step):
             copy.wait_send()
     for copy in started:
@@ -822,6 +830,7 @@
             pltpu.VMEM((6 * ES, LANES), jnp.float32),
             pltpu.VMEM((4, 6 * ES, LANES), jnp.float32),
             pltpu.VMEM((2, ES, LANES), jnp.float32),
+            pltpu.VMEM((2, ES, LANES), jnp.float32),
             pltpu.VMEM((7 * ES, LANES), jnp.float32),
             pltpu.VMEM((2, 7 * ES, LANES), jnp.float32),
             pltpu.VMEM((2, 4 * ES, LANES), jnp.float32),
@@ -829,11 +838,11 @@
             pltpu.VMEM((ROUNDS, 4 * ES, LANES), jnp.float32),
             pltpu.VMEM((ROUNDS, 2, 4 * ES, LANES), jnp.float32),
             pltpu.VMEM((ROUNDS, 2, ES, LANES), jnp.float32),
-            pltpu.VMEM((len(stages), PEERS, 8, LANES), jnp.float32),
+            pltpu.VMEM((len(stages), PEERS, LANES), jnp.float32),
             pltpu.VMEM((7, NP * ES, LANES), jnp.float32),
             pltpu.VMEM((7, A0, A1 * A2), jnp.float32),
-            pltpu.SemaphoreType.DMA((ROUNDS, WAYS)),
-            pltpu.SemaphoreType.DMA((ROUNDS, WAYS)),
+            pltpu.SemaphoreType.DMA((ROUNDS + 1, WAYS)),
+            pltpu.SemaphoreType.DMA((ROUNDS + 1, WAYS)),
             pltpu.SemaphoreType.DMA((len(stages), PEERS)),
             pltpu.SemaphoreType.DMA((len(stages), PEERS)),
         ],

time: 37.8 us -> 35.8 us (0.947)
  Pallas kernels: 35.2 us -> 33.1 us
    pallas_call x1, Pallas kernels: 35.2 us -> 33.1 us  [shards(): pl.pallas_call(functools.partial(kernel, count), out_shape=(block, block)...]
where the time goes in v8:
time: 35.8 us; the launch traced here: 35.6 us
  Pallas kernels  33.1 us (92%)
  local copies, waits for them, and re-layouts  1.87 us (5%)
  between operations  0.65 us (2%)
    pallas_call x1, Pallas kernels, shards(): pl.pallas_call(functools.partial(kernel, count), out_shape=(block, block)...  33.1 us
    unnamed x4, local copies, waits for them, and re-layouts  1.87 us

profile of v8, /device:TPU:0, one launch (start us, length us, event | category | flops | bytes accessed | tf_op | source)
XLA Modules:
  0.0 35.6 jit_solution(869403122059413872)
XLA Ops:
  0.6 0.0 copy-start
  0.6 0.6 %copy-done = s32[16]{0:T(128)S(1)} copy-done((s32[16]{0:T(128)S(1)}, s32[16]{0:T(128)}, u32[]{:S(2)}) %copy-start) | copy-done | bytes 88
  1.3 33.1 %shard_map.86 = (f32[8,896]{1,0:T(8,128)S(1)}, f32[8,896]{1,0:T(8,128)S(1)}) custom-call(f32[3,3,16,512]{3,2,1,0:T(8,128)} %refs_0_.1, f32[2,3,16,512]{3,2,1,0:T(8,128)} %refs_1_.1, f32[3,16,512]{2,1,0:T(8,128)} %refs_2_.1, f32[16,512]{1,0:T(8,128)} %refs_3_.1, s32[1,16]{1,0:T(1,128)S(1)} %bitcast.1, bf16[6144,128]{1,0:T(8,128)(2,1)} %constant.4.clone.refs_5_, ...), custom_call_target="tpu_custom_call" | custom-call | tf_op jit(solution)/shard_map/pallas_call | solution.py:822
  34.4 0.6 %copy.11 = f32[8,896]{1,0:T(8,128)} copy(f32[8,896]{1,0:T(8,128)S(1)} %get-tuple-element.4) | data formatting | bytes 57344
  35.0 0.6 %copy.12 = f32[8,896]{1,0:T(8,128)} copy(f32[8,896]{1,0:T(8,128)S(1)} %get-tuple-element.5) | data formatting | bytes 57344
Async XLA Ops:
  0.6 0.7 %copy-start = (s32[16]{0:T(128)S(1)}, s32[16]{0:T(128)}, u32[]{:S(2)}) copy-start(s32[16]{0:T(128)} %param.11) | copy-start | bytes 196

commit v9 on v8

--- a/solution.py
+++ b/solution.py
@@ -323,7 +323,7 @@
         return me + (other - digit) * stride
 
     barrier = pltpu.get_barrier_semaphore()
-    greeted = [left, right, far_left, far_right, third_left, third_right] + [
+    greeted = ([] if len(stages) == 1 else [left, right, far_left, far_right, third_left, third_right]) + [
         peer(stage, offset)
         for stage in range(len(stages))
         for offset in range(1, stages[stage][1])

time: 35.8 us -> 35.8 us (level)
  no operation moved by 1% of the time
where the time goes in v9:
time: 35.8 us; the launch traced here: 35.6 us
  Pallas kernels  33.1 us (92%)
  local copies, waits for them, and re-layouts  1.87 us (5%)
  between operations  0.65 us (2%)
    pallas_call x1, Pallas kernels, shards(): pl.pallas_call(functools.partial(kernel, count), out_shape=(block, block)...  33.1 us
    unnamed x4, local copies, waits for them, and re-layouts  1.87 us

profile of v9, /device:TPU:0, one launch (start us, length us, event | category | flops | bytes accessed | tf_op | source)
XLA Modules:
  0.0 35.6 jit_solution(4263938134606667100)
XLA Ops:
  0.6 0.0 copy-start
  0.6 0.6 %copy-done = s32[16]{0:T(128)S(1)} copy-done((s32[16]{0:T(128)S(1)}, s32[16]{0:T(128)}, u32[]{:S(2)}) %copy-start) | copy-done | bytes 88
  1.3 33.1 %shard_map.86 = (f32[8,896]{1,0:T(8,128)S(1)}, f32[8,896]{1,0:T(8,128)S(1)}) custom-call(f32[3,3,16,512]{3,2,1,0:T(8,128)} %refs_0_.1, f32[2,3,16,512]{3,2,1,0:T(8,128)} %refs_1_.1, f32[3,16,512]{2,1,0:T(8,128)} %refs_2_.1, f32[16,512]{1,0:T(8,128)} %refs_3_.1, s32[1,16]{1,0:T(1,128)S(1)} %bitcast.1, bf16[6144,128]{1,0:T(8,128)(2,1)} %constant.4.clone.refs_5_, ...), custom_call_target="tpu_custom_call" | custom-call | tf_op jit(solution)/shard_map/pallas_call | solution.py:822
  34.4 0.6 %copy.11 = f32[8,896]{1,0:T(8,128)} copy(f32[8,896]{1,0:T(8,128)S(1)} %get-tuple-element.4) | data formatting | bytes 57344
  35.0 0.6 %copy.12 = f32[8,896]{1,0:T(8,128)} copy(f32[8,896]{1,0:T(8,128)S(1)} %get-tuple-element.5) | data formatting | bytes 57344
Async XLA Ops:
  0.6 0.7 %copy-start = (s32[16]{0:T(128)S(1)}, s32[16]{0:T(128)}, u32[]{:S(2)}) copy-start(s32[16]{0:T(128)} %param.11) | copy-start | bytes 196
